TPU v7x, 256 devices: a whole 4x4x8 slice. The times are simulated.
256 devices in a mesh: section: 2 (over core), dp: 32 (over z, x), head: 4 (over y).
Axes of the slice: x: 4, y: 4, z: 8, core: 2. Of those that a mesh axis runs over, the one named last changes fastest.
Arguments:
- stream: bfloat16 [2, 32, 128, 4096], P(None, 'dp', None, 'head'), may hold values from -6 to 6
- norm_gain: float32 [2, 4096], P('section'), may hold values from 0.1 to 1.9
- w_x: bfloat16 [2, 4096, 4096], P('section', 'dp', 'head'), may hold values from -0.09375 to 0.09375
- w_bc: bfloat16 [2, 4096, 1024], P('section', 'dp', 'head'), may hold values from -0.09375 to 0.09375
- w_dt: bfloat16 [2, 4096, 64], P('section', 'dp', 'head'), may hold values from -0.09375 to 0.09375
- conv_x: float32 [2, 4, 4096], P('section', None, 'head'), may hold values from -3 to 3
- conv_bc: float32 [2, 4, 1024], P('section', None, 'head'), may hold values from -3 to 3
- dt_bias: float32 [2, 64], P('section', 'head'), may hold values from -3 to -1
- decay_rate: float32 [2, 64], P('section', 'head'), may hold values from 0.25 to 16
- skip_d: float32 [2, 64], P('section', 'head'), may hold values from 0.5 to 2
- y_gain: float32 [2, 4096], P('section', 'head'), may hold values from 0.1 to 1.9
- w_out: bfloat16 [2, 4096, 4096], P('section', 'head', 'dp'), may hold values from -0.09375 to 0.09375
Outputs:
- states: bfloat16 [2, 2, 32, 128, 4096], P('section', None, 'dp', None, 'head')
All inputs are finite; a program needn't handle non-finite values.
Results may differ from a plain program's by a relative error of at most 0.018.
Values may be sent and summed in bfloat16 or wider, within the bound.
A program may use at most 64 MiB of HBM per device.

v0:
```python
import jax
import jax.numpy as jnp
from jax import lax
from jax.sharding import PartitionSpec as P

HEAD_DIM = 64
STATE = 128


def shifted(value, axis, steps):
    count = lax.axis_size(axis)
    leading, last = (max(0, -steps), min(count, count - steps))
    return lax.ppermute(value, axis, [(source, source + steps) for source in range(leading, last)])


def causal_conv(values, kernel):
    kernel_width = kernel.shape[0]
    length = values.shape[0]
    padded = jnp.pad(values, ((kernel_width - 1, 0), (0, 0)))
    summed = jnp.zeros_like(values)
    for tap in range(kernel_width):
        summed = summed + kernel[tap] * padded[tap : tap + length, :]
    return jax.nn.silu(summed)


def body(
    stream, norm_gain, w_x, w_bc, w_dt, conv_x, conv_bc, dt_bias, decay_rate, skip_d, y_gain, w_out
):
    in_x, in_bc, in_dt = (
        lax.all_gather(w_x, "dp", axis=1, tiled=True),
        lax.all_gather(w_bc, "dp", axis=1, tiled=True),
        lax.all_gather(w_dt, "dp", axis=1, tiled=True),
    )
    out_full = lax.all_gather(w_out, "dp", axis=2, tiled=True)
    micro_count = stream.shape[0]
    length = stream.shape[2]
    shard_width = stream.shape[3]
    segment_index = lax.axis_index("section")
    tick_count = micro_count + lax.axis_size("section") - 1

    def mixer(features):
        h_float = features.astype(jnp.float32)
        normed = (
            h_float
            * lax.rsqrt(jnp.mean(h_float * h_float, axis=-1, keepdims=True) + 1e-05)
            * norm_gain[0]
        )
        normed = normed.astype(jnp.bfloat16)
        x_proj = jnp.dot(normed, in_x[0], preferred_element_type=jnp.float32)
        bc_proj = jnp.dot(normed, in_bc[0], preferred_element_type=jnp.float32)
        dt_raw = jnp.dot(normed, in_dt[0], preferred_element_type=jnp.float32)
        x_conv = causal_conv(x_proj, conv_x[0])
        bc_conv = causal_conv(bc_proj, conv_bc[0])
        step_size = jax.nn.softplus(dt_raw + dt_bias[0])
        heads_local = step_size.shape[1]
        groups_local = bc_conv.shape[1] // (2 * STATE)
        per_group = heads_local // groups_local
        bc_split = bc_conv.reshape(length, groups_local, 2, STATE)
        b_state = bc_split[:, :, 0, :]
        c_state = bc_split[:, :, 1, :]
        cb_scores = jnp.einsum("tgn,sgn->tsg", c_state, b_state, precision=lax.Precision.HIGHEST)
        decay_sum = jnp.cumsum(step_size * decay_rate[0], axis=0)
        decay_gap = decay_sum[:, None, :] - decay_sum[None, :, :]
        causal_mask = (jnp.arange(length)[:, None] >= jnp.arange(length)[None, :])[:, :, None]
        kernel_mix = jnp.where(causal_mask, jnp.exp(-jnp.where(causal_mask, decay_gap, 0.0)), 0.0)
        kernel_mix = kernel_mix.reshape(length, length, groups_local, per_group)
        mixing = (
            cb_scores[:, :, :, None]
            * kernel_mix
            * step_size.reshape(1, length, groups_local, per_group)
        )
        x_heads = x_conv.reshape(length, groups_local, per_group, HEAD_DIM)
        y_heads = jnp.einsum("tsgj,sgjp->tgjp", mixing, x_heads, precision=lax.Precision.HIGHEST)
        y_heads = y_heads + skip_d[0].reshape(groups_local, per_group)[None, :, :, None] * x_heads
        y_group = y_heads.reshape(length, groups_local, per_group * HEAD_DIM)
        y_group = y_group * lax.rsqrt(jnp.mean(y_group * y_group, axis=-1, keepdims=True) + 1e-05)
        y_normed = (y_group.reshape(length, heads_local * HEAD_DIM) * y_gain[0]).astype(
            jnp.bfloat16
        )
        return jnp.dot(y_normed, out_full[0], preferred_element_type=jnp.float32)

    def skipped(features):
        return jnp.zeros((features.shape[0], out_full.shape[2]), jnp.float32)

    empty_out = jnp.zeros((micro_count, length, shard_width), jnp.bfloat16)
    stream_full = lax.all_gather(stream, "head", axis=3, tiled=True)
    head_index = lax.axis_index("head")

    def step_whole(tick, loop_state):
        inbound, outputs = loop_state
        micro = tick - segment_index
        active = jnp.logical_and(micro >= 0, micro < micro_count)
        micro_at = jnp.clip(micro, 0, micro_count - 1)
        fresh_rows = lax.dynamic_index_in_dim(stream_full, micro_at, 0, keepdims=False)[0]
        features = jnp.where(segment_index == 0, fresh_rows, inbound)
        partial_value = lax.cond(active, mixer, skipped, features)
        summed = lax.psum(partial_value.astype(jnp.bfloat16), "head").astype(jnp.float32)
        updated = (features.astype(jnp.float32) + summed).astype(jnp.bfloat16)
        own_part = lax.dynamic_slice_in_dim(updated, head_index * shard_width, shard_width, 1)
        written = lax.dynamic_update_index_in_dim(outputs, own_part, micro_at, 0)
        outputs = jnp.where(active, written, outputs)
        inbound = shifted(updated, "section", 1)
        return (inbound, outputs)

    start_rows = jnp.zeros((length, shard_width * lax.axis_size("head")), jnp.bfloat16)
    final_state = lax.fori_loop(0, tick_count, step_whole, (start_rows, empty_out))
    return final_state[1][None, :, None]


def solution(mesh):
    in_specs = (
        P(None, "dp", None, "head"),
        P("section", None),
        P("section", "dp", "head"),
        P("section", "dp", "head"),
        P("section", "dp", "head"),
        P("section", None, "head"),
        P("section", None, "head"),
        P("section", "head"),
        P("section", "head"),
        P("section", "head"),
        P("section", "head"),
        P("section", "head", "dp"),
    )
    out_specs = P("section", None, "dp", None, "head")
    return jax.shard_map(body, mesh=mesh, in_specs=in_specs, out_specs=out_specs, check_vma=False)
```

profile of v0, /device:TPU:1, one launch (start us, length us, event | category | flops | bytes accessed | tf_op | source)
XLA Modules:
  0.0 559.9 jit_solution(7313985757580706905)
XLA Ops:
  6.6 0.7 all-gather.5.cloned.1.call-update
  7.4 0.7 all-gather.9.cloned.1.call-update
  8.1 0.7 all-gather.7.cloned.1.call-update
  8.8 0.5 all-gather.11.cloned.1.call-update
  9.4 43.5 %all_gather.18 = bf16[1,4096,16]{1,2,0:T(8,128)(2,1)S(1)} all-gather(bf16[1,128,16]{1,2,0:T(8,128)(2,1)} %param.20), channel_id=1, replica_groups=mesh['section'=2,'dp'=32,'head'=4] {'dp'}, dimensions={1}, use_global_device_ids=true | all-gather | bytes 135168 | tf_op jit(solution)/shard_map/all_gather | solution.py:32
  52.9 70.2 %all-gather.9.cloned.1.call-done = bf16[1,4096,256]{2,1,0:T(8,128)(2,1)} async-done(((bf16[1,128,256]{2,1,0:T(8,128)(2,1)}), bf16[1,4096,256]{2,1,0:T(8,128)(2,1)}) %all-gather.9.cloned.1.call-update) | async-done | bytes 2097168 | tf_op jit(solution)/shard_map/all_gather | solution.py:31
  123.1 101.7 %all-gather.7.cloned.1.call-done = bf16[1,4096,1024]{2,1,0:T(8,128)(2,1)} async-done(((bf16[1,128,1024]{2,1,0:T(8,128)(2,1)}), bf16[1,4096,1024]{2,1,0:T(8,128)(2,1)}) %all-gather.7.cloned.1.call-update) | async-done | bytes 8388624 | tf_op jit(solution)/shard_map/all_gather | solution.py:30
  224.8 101.0 %all-gather.11.cloned.1.call-done = bf16[1,1024,4096]{2,1,0:T(8,128)(2,1)} async-done(((bf16[1,1024,128]{2,1,0:T(8,128)(2,1)}), bf16[1,1024,4096]{2,1,0:T(8,128)(2,1)}) %all-gather.11.cloned.1.call-update) | async-done | bytes 8388624 | tf_op jit(solution)/shard_map/all_gather | solution.py:34
  325.8 0.9 broadcast_in_dim.46
  326.8 226.2 %while.17 = (s32[]{:T(128)}, bf16[128,4096]{1,0:T(8,128)(2,1)S(1)}, bf16[2,128,1024]{2,1,0:T(8,128)(2,1)}, pred[]{:T(512)}, s32[]{:T(128)}, /*index=5*/bf16[2,1,...) while((s32[]{:T(128)}, bf16[128,4096]{1,0:T(8,128)(2,1)S(1)}, ...), condition=%wide.region_7.8_spmd, body=%wide.region_0.7_spmd.sunk | while | flops 2674915584 | bytes 61200580 | solution.py:106
  326.9 1.3 bitcast_select_fusion.3
  328.2 0.1 conditional.2
  328.4 1.0 copy-done
  329.4 65.7 %all-reduce.4.cloned.1.call-done = bf16[128,4096]{1,0:T(8,128)(2,1)} async-done(((bf16[128,4096]{1,0:T(8,128)(2,1)}), bf16[128,4096]{1,0:T(8,128)(2,1)}) %all-reduce.4.cloned.1.call-update) | async-done | bytes 1048592 | tf_op jit(solution)/shard_map/while/body/eval_jaxpr/psum | solution.py:97
  395.2 1.5 add_convert_fusion.2
  396.6 1.3 collective-permute-start
  397.9 1.7 fusion.41
  399.7 2.5 collective-permute-done
  402.1 1.3 bitcast_select_fusion.3
  403.5 16.0 %conditional.2 = (bf16[128,4096]{1,0:T(8,128)(2,1)S(1)}) conditional(s32[]{:T(128)} %convert_element_type.91, () %tuple.52, (f32[1,4,1024]{2,1,0:T(4,128)S(1)}, bf16[128,4096]{1,0:T(8,128)(2,1)S(1)}, f32[1,4096]{1,0:T(1,128)S(1)}, bf16[1,4096,1024]{2,1,0:T(8,128)(2,1)}, f32[1,4,256]{2,1,0:T(4,128)S(1)}, /*index=5*/bf16[1,4096,256]{2,1,0:T(8,128)(2,1)}, ...), branch_computations={%region_1.1_spmd, %region_2.5_spmd} | conditional | flops 2671638784 | bytes 39441652 | solution.py:96
  403.5 0.3 fusion.4
  403.8 4.8 fusion.2
  408.7 0.5 fusion.7
  409.2 0.5 broadcast_multiply_fusion
  409.7 0.6 broadcast.102
  410.2 0.6 reduce.5
  411.1 0.1 fusion.33
  411.3 0.3 convolution_bitcast_fusion.1
  411.7 0.3 divide_multiply_fusion
  412.0 0.2 copy.19
  412.2 0.1 copy.21
  412.3 0.2 reduce_window_sum.10
  412.5 2.1 multiply_reduce_fusion
  414.6 0.2 multiply_convert_fusion
  414.8 4.7 fusion
  419.5 1.0 copy-done
  420.6 50.1 %all-reduce.4.cloned.1.call-done = bf16[128,4096]{1,0:T(8,128)(2,1)} async-done(((bf16[128,4096]{1,0:T(8,128)(2,1)}), bf16[128,4096]{1,0:T(8,128)(2,1)}) %all-reduce.4.cloned.1.call-update) | async-done | bytes 1048592 | tf_op jit(solution)/shard_map/while/body/eval_jaxpr/psum | solution.py:97
  470.6 1.5 add_convert_fusion.2
  472.1 1.3 collective-permute-start
  473.4 1.7 fusion.41
  475.1 2.5 collective-permute-done
  477.6 1.3 bitcast_select_fusion.3
  479.0 16.0 %conditional.2 = (bf16[128,4096]{1,0:T(8,128)(2,1)S(1)}) conditional(s32[]{:T(128)} %convert_element_type.91, () %tuple.52, (f32[1,4,1024]{2,1,0:T(4,128)S(1)}, bf16[128,4096]{1,0:T(8,128)(2,1)S(1)}, f32[1,4096]{1,0:T(1,128)S(1)}, bf16[1,4096,1024]{2,1,0:T(8,128)(2,1)}, f32[1,4,256]{2,1,0:T(4,128)S(1)}, /*index=5*/bf16[1,4096,256]{2,1,0:T(8,128)(2,1)}, ...), branch_computations={%region_1.1_spmd, %region_2.5_spmd} | conditional | flops 2671638784 | bytes 39441652 | solution.py:96
  479.0 0.3 fusion.4
  479.3 4.8 fusion.2
  484.1 0.5 fusion.7
  484.7 0.5 broadcast_multiply_fusion
  485.1 0.6 broadcast.102
  485.7 0.6 reduce.5
  486.6 0.1 fusion.33
  486.7 0.3 convolution_bitcast_fusion.1
  487.2 0.3 divide_multiply_fusion
  487.5 0.2 copy.19
  487.7 0.1 copy.21
  487.8 0.2 reduce_window_sum.10
  488.0 2.1 multiply_reduce_fusion
  490.1 0.2 multiply_convert_fusion
  490.3 4.7 fusion
  495.0 1.0 copy-done
  496.0 50.0 %all-reduce.4.cloned.1.call-done = bf16[128,4096]{1,0:T(8,128)(2,1)} async-done(((bf16[128,4096]{1,0:T(8,128)(2,1)}), bf16[128,4096]{1,0:T(8,128)(2,1)}) %all-reduce.4.cloned.1.call-update) | async-done | bytes 1048592 | tf_op jit(solution)/shard_map/while/body/eval_jaxpr/psum | solution.py:97
  546.1 1.5 add_convert_fusion.2
  547.5 1.3 collective-permute-start
  548.8 1.7 fusion.41
  550.6 2.5 collective-permute-done
  (54 shorter events, 1.3 us)
Async XLA Ops:
  6.5 320.2 %copy-start.4 = (f32[1,1024]{1,0:T(1,128)S(1)}, f32[1,1024]{1,0:T(1,128)}, u32[]{:S(2)}) copy-start(f32[1,1024]{1,0:T(1,128)} %param.26) | copy-start | bytes 12292
  6.5 320.2 %copy-start.8 = (f32[1,16]{1,0:T(1,128)S(1)}, f32[1,16]{1,0:T(1,128)}, u32[]{:S(2)}) copy-start(f32[1,16]{1,0:T(1,128)} %param.25) | copy-start | bytes 196
  6.5 320.2 %copy-start.7 = (f32[1,16]{1,0:T(1,128)S(1)}, f32[1,16]{1,0:T(1,128)}, u32[]{:S(2)}) copy-start(f32[1,16]{1,0:T(1,128)} %param.24) | copy-start | bytes 196
  6.5 320.2 %copy-start.6 = (f32[1,16]{1,0:T(1,128)S(1)}, f32[1,16]{1,0:T(1,128)}, u32[]{:S(2)}) copy-start(f32[1,16]{1,0:T(1,128)} %param.23) | copy-start | bytes 196
  6.5 320.2 %copy-start.3 = (f32[1,4,256]{2,1,0:T(4,128)S(1)}, f32[1,4,256]{2,1,0:T(4,128)}, u32[]{:S(2)}) copy-start(f32[1,4,256]{2,1,0:T(4,128)} %param.22) | copy-start | bytes 12292
  6.5 320.3 %copy-start.2 = (f32[1,4,1024]{2,1,0:T(4,128)S(1)}, f32[1,4,1024]{2,1,0:T(4,128)}, u32[]{:S(2)}) copy-start(f32[1,4,1024]{2,1,0:T(4,128)} %param.21) | copy-start | bytes 49156
  6.6 320.3 %copy-start.1 = (f32[1,4096]{1,0:T(1,128)S(1)}, f32[1,4096]{1,0:T(1,128)}, u32[]{:S(2)}) copy-start(f32[1,4096]{1,0:T(1,128)} %param.17) | copy-start | bytes 49156
  6.6 46.3 %all-gather.5.cloned.1.call-start = ((), (), s32[]{:S(2)}) async-start(), calls=%async_computation | async-start | bytes 2621440 | tf_op jit(solution)/shard_map/all_gather | solution.py:86
  7.3 115.8 %all-gather.9.cloned.1.call-start = ((), (), s32[]{:S(2)}) async-start(), calls=%async_computation.2 | async-start | bytes 2162688 | tf_op jit(solution)/shard_map/all_gather | solution.py:31
  8.1 216.7 %all-gather.7.cloned.1.call-start = ((), (), s32[]{:S(2)}) async-start(), calls=%async_computation.1 | async-start | bytes 8650752 | tf_op jit(solution)/shard_map/all_gather | solution.py:30
  8.8 317.0 %all-gather.11.cloned.1.call-start = ((), (), s32[]{:S(2)}) async-start(), calls=%async_computation.3 | async-start | bytes 8650752 | tf_op jit(solution)/shard_map/all_gather | solution.py:34
  326.8 68.3 %all-reduce.4.cloned.1.call-start = ((), (), s32[]{:S(2)}) async-start(), calls=%async_computation.4 | async-start | bytes 2097152 | tf_op jit(solution)/shard_map/while/body/eval_jaxpr/psum | solution.py:97
  328.4 1.0 copy-start
  396.6 5.5 collective-permute-start
  402.1 68.5 %all-reduce.4.cloned.1.call-start = ((), (), s32[]{:S(2)}) async-start(), calls=%async_computation.4 | async-start | bytes 2097152 | tf_op jit(solution)/shard_map/while/body/eval_jaxpr/psum | solution.py:97
  403.8 4.8 copy-start.5
  419.5 1.0 copy-start
  472.1 5.5 collective-permute-start
  477.6 68.4 %all-reduce.4.cloned.1.call-start = ((), (), s32[]{:S(2)}) async-start(), calls=%async_computation.4 | async-start | bytes 2097152 | tf_op jit(solution)/shard_map/while/body/eval_jaxpr/psum | solution.py:97
  479.3 4.8 copy-start.5
  495.0 1.0 copy-start
  547.5 5.5 collective-permute-start
Sparse Core Ops, SparseCore 0:
  9.2 37.2 all-gather.4
  49.0 73.9 all-gather.8
  125.7 99.0 all-gather.6
  227.1 98.6 all-gather.10
  329.7 65.3 all-reduce.3
  420.7 49.9 all-reduce.3
  496.1 49.8 all-reduce.3
where the time goes:
time: 560 us
  waiting for transfers between devices  449 us (80%)
  blocking collectives  43.5 us (8%)
  matrix products  25.7 us (5%)
  other arithmetic  17.1 us (3%)
  between operations  13.5 us (2%)
  local copies, waits for them, and re-layouts  6.65 us (1%)
    psum x3, waiting for transfers between devices, step_whole(): lax.psum(partial_value.astype(jnp.bfloat16), 'head').astype(jnp.float32)  166 us
    all_gather x1, waiting for transfers between devices, body(): lax.all_gather(w_x, 'dp', axis=1, tiled=True)  102 us
    all_gather x1, waiting for transfers between devices, body(): out_full = lax.all_gather(w_out, 'dp', axis=2, tiled=True)  101 us
    all_gather x1, waiting for transfers between devices, body(): lax.all_gather(w_bc, 'dp', axis=1, tiled=True)  70.2 us
    all_gather x1, blocking collectives, body(): lax.all_gather(w_dt, 'dp', axis=1, tiled=True)  43.5 us
  transfers between devices with their start and end apart: 10, of which 9 were waited for; matrix products, arithmetic and copies ran while one was open for 1% of the time, Pallas kernels for 0%

commit v1 on v0

v1 whole, which is shorter than its diff:
```python
import functools

import jax
import jax.numpy as jnp
from jax import lax
from jax.experimental import pallas as pl
from jax.experimental.pallas import tpu as pltpu
from jax.sharding import PartitionSpec as P

MESH = pl.DeviceIdType.MESH
HEAD_DIM = 64
STATE = 128
NX = 4
NY = 4
NZ = 8
MICRO = 2
LEN = 128
ROWS = NX * LEN
WIDTH = 1024
BC = 2 * STATE
COLS = WIDTH + BC + 128
HALF = 64
EPS = 1e-05
F32 = jnp.float32
BF16 = jnp.bfloat16


def remote(src, dst, send_sem, recv_sem, device):
    return pltpu.make_async_remote_copy(
        src_ref=src,
        dst_ref=dst,
        send_sem=send_sem,
        recv_sem=recv_sem,
        device_id=device,
        device_id_type=MESH,
    )


def kernel(
    stream_ref,
    w_in_ref,
    w_out_ref,
    par_ref,
    out_ref,
    staged,
    w_in,
    w_out,
    act,
    scaled,
    part,
    got,
    padded,
    conv,
    y_raw,
    y_all,
    proj,
    proj_got,
    h_next,
    squares,
    in_send,
    in_recv,
    wout_send,
    wout_recv,
    first_send,
    first_recv,
    next_send,
    next_recv,
    part_send,
    part_recv,
    y_send,
    y_recv,
    proj_send,
    proj_recv,
    out_send,
    out_recv,
    go_sem,
):
    section = lax.axis_index("section")
    dp = lax.axis_index("dp")
    y = lax.axis_index("head")
    z = dp // NX
    x = dp % NX

    def at(s, zz, xx, yy):
        return (s, zz * NX + xx, yy)

    right, left = (z + 1) % NZ, (z + NZ - 1) % NZ

    barrier = pltpu.get_barrier_semaphore()
    for dx in range(NX):
        for dy in range(NY):
            if dx or dy:
                pl.semaphore_signal(
                    barrier,
                    inc=1,
                    device_id=at(section, z, (x + dx) % NX, (y + dy) % NY),
                    device_id_type=MESH,
                )
    for dy in range(NY):
        pl.semaphore_signal(
            barrier, inc=1, device_id=at(1 - section, z, x, (y + dy) % NY), device_id_type=MESH
        )
    for zz in (right, left):
        pl.semaphore_signal(
            barrier, inc=1, device_id=at(section, zz, x, y), device_id_type=MESH
        )
    pl.semaphore_wait(barrier, NX * NY - 1 + NY + 2)

    def in_hop(direction, step, half):
        owner = (z + NZ - step) % NZ if direction == 0 else (z + step) % NZ
        rows = (
            pl.ds(pl.multiple_of(owner * LEN, LEN), LEN)
            if not half
            else pl.ds(pl.multiple_of(owner * LEN + direction * HALF, HALF), HALF)
        )
        src = w_in.at[rows]
        return remote(
            src,
            src,
            in_send.at[direction, step],
            in_recv.at[direction, step],
            at(section, right if direction == 0 else left, x, y),
        )

    def out_hop(direction, step, half):
        owner = (z + NZ - step) % NZ if direction == 0 else (z + step) % NZ
        columns = pl.ds(pl.multiple_of(owner * LEN, LEN), LEN)
        src = (
            w_out.at[:, columns]
            if not half
            else w_out.at[pl.ds(direction * (WIDTH // 2), WIDTH // 2), columns]
        )
        return remote(
            src,
            src,
            wout_send.at[direction, step],
            wout_recv.at[direction, step],
            at(section, right if direction == 0 else left, x, y),
        )

    def ring_start(hop):
        for direction in range(2):
            hop(direction, 0, False).start()

    def ring_step(hop, step, last):
        for direction in range(2):
            hop(direction, step - 1, False).wait_recv()
            hop(direction, step, last).start()

    def ring_end(hop):
        for direction in range(2):
            hop(direction, 3, True).wait_recv()

    own_rows = pl.ds(pl.multiple_of(z * LEN, LEN), LEN)
    w_in[own_rows, :] = w_in_ref[...]
    w_out[:, own_rows] = w_out_ref[0]

    @pl.when(section == 1)
    def _():
        pl.semaphore_wait(go_sem, 1)

    ring_start(in_hop)

    def first(m, dx, dy):
        to_x = (x + dx) % NX
        to_y = (y + dy) % NY
        return remote(
            staged.at[m, to_x],
            act.at[m, y, pl.ds(pl.multiple_of(x * LEN, LEN), LEN), :],
            first_send.at[m, dx, dy],
            first_recv.at[m, dx, dy],
            at(0, z, to_x, to_y),
        )

    @pl.when(section == 0)
    def _():
        for m in range(MICRO):
            for xx in range(NX):
                staged[m, xx, :, :LEN] = stream_ref[m, 0, :, xx * LEN : (xx + 1) * LEN]
                staged[m, xx, :, LEN:] = stream_ref[
                    m, 0, :, (xx + NX) * LEN : (xx + NX + 1) * LEN
                ]
            act[m, y, pl.ds(pl.multiple_of(x * LEN, LEN), LEN), :] = staged[m, x]
            for dx in range(NX):
                for dy in range(NY):
                    if dx or dy:
                        first(m, dx, dy).start()

    for step in range(1, 4):
        ring_step(in_hop, step, step == 3)
    ring_end(in_hop)

    @pl.when(section == 0)
    def _():
        pl.semaphore_signal(go_sem, inc=1, device_id=at(1, z, x, y), device_id_type=MESH)

    ring_start(out_hop)

    def onward(m, dy):
        return remote(
            h_next.at[m],
            act.at[m, y],
            next_send.at[m, dy],
            next_recv.at[m, dy],
            at(1 - section, z, x, (y + dy) % NY),
        )

    def send_part(m, dx):
        to_x = (x + dx) % NX
        return remote(
            part.at[m, pl.ds(pl.multiple_of(to_x * LEN, LEN), LEN), :],
            got.at[m, dx],
            part_send.at[m, dx],
            part_recv.at[m, dx],
            at(section, z, to_x, y),
        )

    def send_y(m, dx):
        return remote(
            y_all.at[m, x],
            y_all.at[m, x],
            y_send.at[m, dx],
            y_recv.at[m, dx],
            at(section, z, (x + dx) % NX, y),
        )

    def send_proj(m, dy):
        to_y = (y + dy) % NY
        return remote(
            proj.at[m, to_y],
            proj_got.at[m, dy],
            proj_send.at[m, dy],
            proj_recv.at[m, dy],
            at(section, z, x, to_y),
        )

    def send_out(m, dx, part_of):
        to_x = (x + dx) % NX
        return remote(
            h_next.at[
                m,
                pl.ds(pl.multiple_of(to_x * LEN, LEN), LEN),
                part_of * LEN : (part_of + 1) * LEN,
            ],
            out_ref.at[
                0, m, 0, :, pl.ds(pl.multiple_of((x + NX * part_of) * LEN, LEN), LEN)
            ],
            out_send.at[m, dx, part_of],
            out_recv.at[m, dx, part_of],
            at(section, z, to_x, y),
        )

    lane = lax.broadcasted_iota(jnp.int32, (LEN, LEN), 1)
    row = lax.broadcasted_iota(jnp.int32, (LEN, LEN), 0)

    def project_in(m):
        @pl.when(section == 0)
        def _():
            for dx in range(NX):
                for dy in range(NY):
                    if dx or dy:
                        first(m, dx, dy).wait_recv()

        @pl.when(section == 1)
        def _():
            for dy in range(NY):
                onward(m, dy).wait_recv()

        def scale(i, carry):
            rows = pl.ds(pl.multiple_of(i * 64, 64), 64)
            total = jnp.zeros((64, LEN), F32)
            for yy in range(NY):
                for half in range(2):
                    at_ = yy * 2 * LEN + half * LEN
                    value = act[m, yy, rows, half * LEN : (half + 1) * LEN].astype(F32)
                    total = total + value * value
                    gain = par_ref[8 + x, :, at_ : at_ + LEN]
                    scaled[rows, at_ : at_ + LEN] = (value * gain).astype(BF16)
            squares[rows, :] = jnp.broadcast_to(jnp.sum(total, axis=1, keepdims=True), (64, LEN))
            return carry

        lax.fori_loop(0, ROWS // 64, scale, 0)

        def columns(i, carry):
            cols = pl.ds(pl.multiple_of(i * 256, 256), 256)
            part[m, :, cols] = jnp.dot(
                scaled[...], w_in[:, cols], preferred_element_type=F32
            ).astype(BF16)
            return carry

        lax.fori_loop(0, (WIDTH + BC) // 256, columns, 0)
        small = jnp.dot(scaled[...], w_in[:, WIDTH + BC :], preferred_element_type=F32)
        high = small.astype(BF16).astype(F32)
        low = small - high
        square = squares[...]
        square_high = square.astype(BF16).astype(F32)
        lanes = lax.broadcasted_iota(jnp.int32, (ROWS, LEN), 1)
        packed = high + pltpu.roll(low, 16, 1)
        packed = jnp.where(lanes == 32, square_high, packed)
        packed = jnp.where(lanes == 33, square - square_high, packed)
        part[m, :, WIDTH + BC :] = packed.astype(BF16)
        for dx in (1, 3, 2):
            send_part(m, dx).start()

    def mix(m):
        for dx in (1, 3, 2):
            send_part(m, dx).wait_recv()
        own = pl.ds(pl.multiple_of(x * LEN, LEN), LEN)

        def summed(cols):
            total = part[m, own, cols].astype(F32)
            for dx in (1, 2, 3):
                total = total + got[m, dx, :, cols].astype(F32)
            return total

        tail = summed(slice(WIDTH + BC, COLS))
        square = tail[:, 32:33] + tail[:, 33:34]
        inverse = lax.rsqrt(square * (1.0 / (NX * WIDTH)) + EPS)
        raw = (tail + pltpu.roll(tail, LEN - 16, 1)) * inverse
        pre = raw + par_ref[6, :, :LEN]
        steps = jnp.maximum(pre, 0.0) + jnp.log1p(jnp.exp(-jnp.abs(pre)))
        steps = jnp.where(lane < 16, steps, 0.0)
        lower = jnp.where(row >= lane, 1.0, 0.0)
        decay = jnp.dot(
            lower,
            steps * par_ref[7, :, :LEN],
            precision=lax.Precision.HIGHEST,
            preferred_element_type=F32,
        )
        decay_t = decay.T
        inverse_wide = jnp.broadcast_to(inverse, (LEN, LEN))

        padded[0:8, :] = jnp.zeros((8, LEN), F32)

        for c in range((WIDTH + BC) // LEN):
            cols = slice(c * LEN, (c + 1) * LEN)
            padded[8:, :] = summed(cols) * inverse_wide
            value = jnp.zeros((LEN, LEN), F32)
            for tap in range(4):
                value = value + par_ref[tap, :, cols] * padded[5 + tap : 5 + tap + LEN, :]
            conv[:, cols] = value / (1.0 + jnp.exp(-value))

        scores = lax.dot_general(
            conv[:, WIDTH + STATE : WIDTH + BC],
            conv[:, WIDTH : WIDTH + STATE],
            (((1,), (1,)), ((), ())),
            precision=lax.Precision.HIGHEST,
            preferred_element_type=F32,
        )
        scores = jnp.where(row >= lane, scores, 0.0)
        power = jnp.zeros((LEN, LEN), F32)
        for pair in range(WIDTH // LEN):
            cols = slice(pair * LEN, (pair + 1) * LEN)
            mixes = []
            for j in (2 * pair, 2 * pair + 1):
                gap = jnp.minimum(decay_t[j : j + 1, :] - decay[:, j : j + 1], 0.0)
                mixes.append((jnp.exp(gap) * scores).astype(BF16))
            value = conv[:, cols]
            step = jnp.where(
                lane < HEAD_DIM,
                steps[:, 2 * pair : 2 * pair + 1],
                steps[:, 2 * pair + 1 : 2 * pair + 2],
            )
            stepped = value * step
            blocks = jnp.concatenate(
                [
                    jnp.where(lane < HEAD_DIM, stepped, 0.0).astype(BF16),
                    jnp.where(lane < HEAD_DIM, 0.0, stepped).astype(BF16),
                ],
                axis=0,
            )
            mixed = jnp.dot(
                jnp.concatenate(mixes, axis=1), blocks, preferred_element_type=F32
            )
            mixed = mixed + par_ref[5, :, cols] * value
            power = power + mixed * mixed
            y_raw[:, cols] = mixed
        norm = lax.rsqrt(jnp.sum(power, axis=1, keepdims=True) * (1.0 / WIDTH) + EPS)
        norm = jnp.broadcast_to(norm, (LEN, LEN))
        for c in range(WIDTH // LEN):
            cols = slice(c * LEN, (c + 1) * LEN)
            y_all[m, x, :, cols] = (y_raw[:, cols] * norm * par_ref[4, :, cols]).astype(BF16)
        for dx in (1, 3, 2):
            send_y(m, dx).start()

    def project_out(m):
        for dx in (1, 3, 2):
            send_y(m, dx).wait_recv()

        values = y_all[m].reshape(ROWS, WIDTH)
        for dy in (1, 3, 2, 0):
            to_y = (y + dy) % NY
            cols = pl.ds(pl.multiple_of(to_y * 2 * LEN, 2 * LEN), 2 * LEN)
            proj[m, to_y] = jnp.dot(
                values, w_out[:, cols], preferred_element_type=F32
            ).astype(BF16)
            if dy:
                send_proj(m, dy).start()

    def finish(m):
        for dy in (1, 3, 2):
            send_proj(m, dy).wait_recv()

        def add(i, carry):
            rows = pl.ds(pl.multiple_of(i * 64, 64), 64)
            total = proj[m, y, rows, :].astype(F32)
            for dy in (1, 2, 3):
                total = total + proj_got[m, dy, rows, :].astype(F32)
            h_next[m, rows, :] = (act[m, y, rows, :].astype(F32) + total).astype(BF16)
            return carry

        lax.fori_loop(0, ROWS // 64, add, 0)

        @pl.when(section == 0)
        def _():
            for dy in (1, 3, 2, 0):
                onward(m, dy).start()

        for dx in (1, 3, 2):
            for part_of in range(2):
                send_out(m, dx, part_of).start()
        own = pl.ds(pl.multiple_of(x * LEN, LEN), LEN)
        for part_of in range(2):
            out_ref[
                0, m, 0, :, pl.ds(pl.multiple_of((x + NX * part_of) * LEN, LEN), LEN)
            ] = h_next[m, own, part_of * LEN : (part_of + 1) * LEN]

    def stage_in(m, carry):
        project_in(m)
        ring_step(out_hop, m + 1, False)
        return carry

    def stage_mix(m, carry):
        mix(m)
        return carry

    def stage_out(m, carry):
        project_out(m)
        return carry

    def stage_end(m, carry):
        finish(m)
        return carry

    lax.fori_loop(0, MICRO, stage_in, 0)
    ring_step(out_hop, 3, True)
    lax.fori_loop(0, MICRO, stage_mix, 0)
    ring_end(out_hop)
    lax.fori_loop(0, MICRO, stage_out, 0)
    lax.fori_loop(0, MICRO, stage_end, 0)

    def drain(m, carry):
        for dx in (1, 2, 3):
            for part_of in range(2):
                send_out(m, dx, part_of).wait()
            send_part(m, dx).wait_send()
            send_y(m, dx).wait_send()
        for dy in (1, 2, 3):
            send_proj(m, dy).wait_send()

        @pl.when(section == 0)
        def _():
            for dy in range(NY):
                onward(m, dy).wait_send()
            for dx in range(NX):
                for dy in range(NY):
                    if dx or dy:
                        first(m, dx, dy).wait_send()

        return carry

    lax.fori_loop(0, MICRO, drain, 0)
    for step in range(4):
        for direction in range(2):
            in_hop(direction, step, step == 3).wait_send()
            out_hop(direction, step, step == 3).wait_send()


def body(
    stream, norm_gain, w_x, w_bc, w_dt, conv_x, conv_bc, dt_bias, decay_rate, skip_d, y_gain, w_out
):
    w_in = jnp.concatenate(
        [w_x[0], w_bc[0], jnp.pad(w_dt[0], ((0, 0), (0, 128 - w_dt.shape[2])))], axis=1
    )

    def wide(rows):
        return jnp.pad(rows, ((0, 0), (0, COLS - rows.shape[1])))

    gains = norm_gain[0].reshape(NZ, NX, LEN).transpose(1, 0, 2).reshape(NX, WIDTH)
    params = jnp.concatenate(
        [
            wide(jnp.concatenate([conv_x[0], conv_bc[0]], axis=1)),
            wide(y_gain),
            wide(jnp.repeat(skip_d, HEAD_DIM, axis=1)),
            wide(dt_bias),
            wide(decay_rate),
            wide(gains),
        ],
        axis=0,
    ).reshape(8 + NX, 1, COLS)
    vmem = pl.BlockSpec(memory_space=pltpu.VMEM)
    dma = pltpu.SemaphoreType.DMA
    return pl.pallas_call(
        kernel,
        out_shape=jax.ShapeDtypeStruct((1, MICRO, 1, LEN, WIDTH), BF16),
        in_specs=[vmem] * 4,
        out_specs=vmem,
        scratch_shapes=[
            pltpu.VMEM((MICRO, NX, LEN, 2 * LEN), BF16),
            pltpu.VMEM((NZ * LEN, COLS), BF16),
            pltpu.VMEM((WIDTH, NZ * LEN), BF16),
            pltpu.VMEM((MICRO, NY, ROWS, 2 * LEN), BF16),
            pltpu.VMEM((ROWS, WIDTH), BF16),
            pltpu.VMEM((MICRO, ROWS, COLS), BF16),
            pltpu.VMEM((MICRO, NX, LEN, COLS), BF16),
            pltpu.VMEM((8 + LEN, LEN), F32),
            pltpu.VMEM((LEN, WIDTH + BC), F32),
            pltpu.VMEM((LEN, WIDTH), F32),
            pltpu.VMEM((MICRO, NX, LEN, WIDTH), BF16),
            pltpu.VMEM((MICRO, NY, ROWS, 2 * LEN), BF16),
            pltpu.VMEM((MICRO, NY, ROWS, 2 * LEN), BF16),
            pltpu.VMEM((MICRO, ROWS, 2 * LEN), BF16),
            pltpu.VMEM((ROWS, LEN), F32),
            dma((2, 4)),
            dma((2, 4)),
            dma((2, 4)),
            dma((2, 4)),
            dma((MICRO, NX, NY)),
            dma((MICRO, NX, NY)),
            dma((MICRO, NY)),
            dma((MICRO, NY)),
            dma((MICRO, NX)),
            dma((MICRO, NX)),
            dma((MICRO, NX)),
            dma((MICRO, NX)),
            dma((MICRO, NY)),
            dma((MICRO, NY)),
            dma((MICRO, NX, 2)),
            dma((MICRO, NX, 2)),
            pltpu.SemaphoreType.REGULAR,
        ],
        compiler_params=pltpu.CompilerParams(
            collective_id=0, has_side_effects=True, vmem_limit_bytes=48 * 1024 * 1024
        ),
        name="mixer",
    )(stream, w_in, w_out, params)


def solution(mesh):
    in_specs = (
        P(None, "dp", None, "head"),
        P("section", None),
        P("section", "dp", "head"),
        P("section", "dp", "head"),
        P("section", "dp", "head"),
        P("section", None, "head"),
        P("section", None, "head"),
        P("section", "head"),
        P("section", "head"),
        P("section", "head"),
        P("section", "head"),
        P("section", "head", "dp"),
    )
    out_specs = P("section", None, "dp", None, "head")
    return jax.shard_map(body, mesh=mesh, in_specs=in_specs, out_specs=out_specs, check_vma=False)
```

time: 560 us -> 146 us (0.26)
  waiting for transfers between devices: 449 us -> 0 us
  Pallas kernels: 0 us -> 140 us
  blocking collectives: 43.5 us -> 0 us
  matrix products: 25.7 us -> 0 us
  other arithmetic: 17.1 us -> 0.04 us
  between operations: 13.5 us -> 0.09 us
    all_gather x4 -> x0, waiting for transfers between devices: 273 us -> none  [the longest x1 102 us: body(): lax.all_gather(w_x, 'dp', axis=1, tiled=True)]
    psum x3 -> x0, waiting for transfers between devices: 166 us -> none  [step_whole(): lax.psum(partial_value.astype(jnp.bfloat16), 'head').astype(jnp.float32)]
    pallas_call x0 -> x1, Pallas kernels: none -> 140 us  [body(): pl.pallas_call(kernel, out_shape=jax.ShapeDtypeStruct((1, MICRO, 1, LEN,...]
    all_gather x1 -> x0, blocking collectives: 43.5 us -> none  [body(): lax.all_gather(w_dt, 'dp', axis=1, tiled=True)]
    dot_general x12 -> x0, matrix products: 25.7 us -> none  [the longest x2 9.65 us: mixer(): x_proj = jnp.dot(normed, in_x[0], preferred_element_type=jnp.float32)]
    select_n x6 -> x0, other arithmetic: 9.2 us -> none  [the longest x3 5.18 us: step_whole(): outputs = jnp.where(active, written, outputs)]
    ppermute x3 -> x0, waiting for transfers between devices: 7.45 us -> none  [shifted(): lax.ppermute(value, axis, [(source, source + steps) for source in range(l...]
    unnamed x14 -> x27, local copies, waits for them, and re-layouts: 0.03 us -> 5.66 us
  transfers between devices with their start and end apart: 10 -> 0, of which waited for: 9 -> 0; matrix products, arithmetic and copies ran while one was open for 1% -> 0% of each run, Pallas kernels for 0% -> 0%
where the time goes in v1:
time: 146 us
  Pallas kernels  140 us (96%)
  local copies, waits for them, and re-layouts  5.96 us (4%)
    pallas_call x1, Pallas kernels, body(): pl.pallas_call(kernel, out_shape=jax.ShapeDtypeStruct((1, MICRO, 1, LEN,...  140 us
    unnamed x27, local copies, waits for them, and re-layouts  5.66 us

profile of v1, /device:TPU:1, one launch (start us, length us, event | category | flops | bytes accessed | tf_op | source)
XLA Modules:
  0.0 145.7 jit_solution(4764166801791478477)
XLA Ops:
  0.0 0.0 copy-start.10
  0.0 0.7 copy-done.10
  0.7 0.0 copy-start.11
  0.7 0.6 copy-done.11
  1.3 0.0 copy-start.7
  1.3 0.7 copy-done.7
  2.0 0.0 copy-start.9
  2.0 0.6 copy-done.9
  2.7 0.0 copy-start.4
  2.7 0.0 copy-start.5
  2.7 0.0 copy-start.8
  2.7 0.1 broadcast_in_dim.5
  2.7 0.0 copy-start.2
  2.7 0.1 broadcast_in_dim.6
  2.8 0.5 copy-done.4
  3.4 0.0 copy-done.5
  3.4 0.0 copy-done.8
  3.4 0.0 copy-start.6
  3.4 0.0 copy-start.3
  3.5 0.0 copy-start
  3.5 0.1 concatenate.11
  3.6 0.5 copy-done.6
  4.1 0.1 copy.13
  4.2 0.0 copy-done.2
  4.2 0.1 copy-done.3
  4.3 0.0 copy-start.1
  4.3 0.2 copy-done
  4.5 0.7 copy-done.1
  5.3 139.6 %mixer.1 = bf16[1,2,1,128,1024]{4,3,2,1,0:T(8,128)(2,1)S(1)} custom-call(bf16[2,1,128,1024]{3,2,1,0:T(8,128)(2,1)S(1)} %copy-done, bf16[128,1408]{1,0:T(8,128)(2,1)S(1)} %fusion.1.w_in_ref, bf16[1,1024,128]{2,1,0:T(8,128)(2,1)S(1)} %copy-done.1, f32[12,1,1408]{2,1,0:T(1,128)S(1)} %reshape.12.par_ref), custom_call_target="tpu_custom_call" | custom-call | tf_op jit(solution)/shard_map/mixer/pallas_call | solution.py:503
  144.9 0.8 copy.21
  (10 shorter events, 0.1 us)
Async XLA Ops:
  0.0 0.7 copy-start.10
  0.7 0.7 copy-start.11
  1.3 0.7 copy-start.7
  2.0 0.7 copy-start.9
  2.7 0.7 copy-start.4
  2.7 0.7 copy-start.5
  2.7 0.7 copy-start.8
  2.7 1.5 %copy-start.2 = (bf16[1,128,1024]{2,1,0:T(8,128)(2,1)S(1)}, bf16[1,128,1024]{2,1,0:T(8,128)(2,1)}, u32[]{:S(2)}) copy-start(bf16[1,128,1024]{2,1,0:T(8,128)(2,1)} %param.14) | copy-start | bytes 786436
  3.4 0.7 copy-start.6
  3.4 0.9 copy-start.3
  3.5 1.1 copy-start
  4.3 1.0 copy-start.1

commit v2 on v1

v2 whole, which is shorter than its diff:
```python
import functools

import jax
import jax.numpy as jnp
from jax import lax
from jax.experimental import pallas as pl
from jax.experimental.pallas import tpu as pltpu
from jax.sharding import PartitionSpec as P

MESH = pl.DeviceIdType.MESH
HEAD_DIM = 64
STATE = 128
NX = 4
NY = 4
NZ = 8
MICRO = 2
LEN = 128
ROWS = NX * LEN
WIDTH = 1024
BC = 2 * STATE
COLS = WIDTH + BC + 128
CHUNKS = 4
EPS = 1e-05
F32 = jnp.float32
BF16 = jnp.bfloat16


def remote(src, dst, send_sem, recv_sem, device):
    return pltpu.make_async_remote_copy(
        src_ref=src,
        dst_ref=dst,
        send_sem=send_sem,
        recv_sem=recv_sem,
        device_id=device,
        device_id_type=MESH,
    )


def kernel(
    stream_ref,
    gain_ref,
    w_x_ref,
    w_bc_ref,
    w_dt_ref,
    conv_x_ref,
    conv_bc_ref,
    bias_ref,
    rate_ref,
    skip_ref,
    y_gain_ref,
    w_out_ref,
    out_ref,
    staged,
    gains,
    w_dt,
    taps,
    biases,
    rates,
    skips,
    y_gains,
    w_in,
    w_out,
    relay,
    act,
    scaled,
    part,
    got,
    padded,
    conv,
    y_raw,
    y_all,
    proj,
    proj_got,
    h_next,
    squares,
    in_send,
    in_recv,
    wout_send,
    wout_recv,
    first_send,
    first_recv,
    next_send,
    next_recv,
    part_send,
    part_recv,
    y_send,
    y_recv,
    proj_send,
    proj_recv,
    out_send,
    out_recv,
    relay_send,
    relay_recv,
    push_send,
    push_recv,
    own_send,
    own_recv,
    load_sem,
    stream_sem,
    go_sem,
):
    section = lax.axis_index("section")
    dp = lax.axis_index("dp")
    y = lax.axis_index("head")
    z = dp // NX
    x = dp % NX

    def at(s, zz, xx, yy):
        return (s, zz * NX + xx, yy)

    right, left = (z + 1) % NZ, (z + NZ - 1) % NZ
    sibling = at(1 - section, z, x, y)
    own_block = pl.ds(pl.multiple_of(z * LEN, LEN), LEN)

    loads = [
        pltpu.make_async_copy(source, target, load_sem.at[i])
        for i, (source, target) in enumerate(
            [
                (w_out_ref.at[0], w_out.at[:, own_block]),
                (w_x_ref.at[0], w_in.at[own_block, :WIDTH]),
                (w_bc_ref.at[0], w_in.at[own_block, WIDTH : WIDTH + BC]),
                (w_dt_ref.at[0], w_dt),
                (gain_ref, gains),
                (conv_x_ref.at[0], taps.at[:, :WIDTH]),
                (conv_bc_ref.at[0], taps.at[:, WIDTH:]),
                (bias_ref, biases),
                (rate_ref, rates),
                (skip_ref, skips),
                (y_gain_ref, y_gains),
            ]
        )
    ]
    for load in loads:
        load.start()

    def stage(m, xx, half):
        return pltpu.make_async_copy(
            stream_ref.at[m, 0, :, pl.ds((xx + NX * half) * LEN, LEN)],
            staged.at[m, xx, :, pl.ds(half * LEN, LEN)],
            stream_sem.at[m, xx, half],
        )

    @pl.when(section == 0)
    def _():
        for m in range(MICRO):
            for xx in range(NX):
                for half in range(2):
                    stage(m, xx, half).start()

    barrier = pltpu.get_barrier_semaphore()
    for dx in range(NX):
        for dy in range(NY):
            if dx or dy:
                pl.semaphore_signal(
                    barrier,
                    inc=1,
                    device_id=at(section, z, (x + dx) % NX, (y + dy) % NY),
                    device_id_type=MESH,
                )
    for dy in range(NY):
        pl.semaphore_signal(
            barrier, inc=1, device_id=at(1 - section, z, x, (y + dy) % NY), device_id_type=MESH
        )
    for zz in (right, left):
        pl.semaphore_signal(
            barrier, inc=1, device_id=at(section, zz, x, y), device_id_type=MESH
        )
    pl.semaphore_wait(barrier, NX * NY - 1 + NY + 2)

    def hop(buffer, by_rows, sends, receives):
        def one(direction, step, chunk):
            owner = (z + NZ - step) % NZ if direction == 0 else (z + step) % NZ
            if by_rows:
                size = LEN // CHUNKS
                piece = buffer.at[pl.ds(pl.multiple_of(owner * LEN + chunk * size, size), size)]
            else:
                size = WIDTH // CHUNKS
                piece = buffer.at[
                    pl.ds(chunk * size, size), pl.ds(pl.multiple_of(owner * LEN, LEN), LEN)
                ]
            return remote(
                piece,
                piece,
                sends.at[direction, step, chunk],
                receives.at[direction, step, chunk],
                at(section, right if direction == 0 else left, x, y),
            )

        return one

    in_hop = hop(w_in, True, in_send, in_recv)
    out_hop = hop(w_out, False, wout_send, wout_recv)
    relay_hop = hop(relay, False, relay_send, relay_recv)

    def pieces(step):
        half = CHUNKS // 2
        return [
            (chunk, direction)
            for chunk in range(CHUNKS)
            for direction in range(2)
            if step < 3 or chunk // half == direction
        ]

    def ring_start(one):
        for chunk, direction in pieces(0):
            one(direction, 0, chunk).start()

    def ring_middle(one, arrived=None):
        for step in range(1, 4):
            for chunk, direction in pieces(0):
                one(direction, step - 1, chunk).wait_recv()
                if (chunk, direction) in pieces(step):
                    one(direction, step, chunk).start()
            if arrived is not None:
                arrived(step)

    def ring_end(one):
        for chunk, direction in pieces(3):
            one(direction, 3, chunk).wait_recv()

    def ring_drain(one):
        for step in range(4):
            for chunk, direction in pieces(step):
                one(direction, step, chunk).wait_send()

    def own_out():
        return remote(
            w_out.at[:, own_block], relay.at[:, own_block], own_send, own_recv, sibling
        )

    def push(step):
        columns = pl.ds(pl.multiple_of((z + step) % NZ * LEN, LEN), LEN)
        return remote(
            relay.at[:, columns],
            w_out.at[:, columns],
            push_send.at[step],
            push_recv.at[step],
            sibling,
        )

    def push_both(step):
        push(step).start()
        push(NZ - step).start()

    loads[0].wait()

    @pl.when(section == 0)
    def _():
        own_out().start()

    for load in loads[1:]:
        load.wait()
    w_in[own_block, WIDTH + BC :] = jnp.concatenate(
        [w_dt[...], jnp.zeros((LEN, LEN - 16), BF16)], axis=1
    )

    def first(m, dx, dy):
        to_x = (x + dx) % NX
        to_y = (y + dy) % NY
        return remote(
            staged.at[m, to_x],
            act.at[m, y, pl.ds(pl.multiple_of(x * LEN, LEN), LEN), :],
            first_send.at[m, dx, dy],
            first_recv.at[m, dx, dy],
            at(0, z, to_x, to_y),
        )

    @pl.when(section == 0)
    def _():
        ring_start(in_hop)
        for m in range(MICRO):
            for xx in range(NX):
                for half in range(2):
                    stage(m, xx, half).wait()
            act[m, y, pl.ds(pl.multiple_of(x * LEN, LEN), LEN), :] = staged[m, x]
            for dx in range(NX):
                for dy in range(NY):
                    if dx or dy:
                        first(m, dx, dy).start()
        ring_middle(in_hop)
        pl.semaphore_signal(go_sem, inc=1, device_id=sibling, device_id_type=MESH)

    @pl.when(section == 1)
    def _():
        own_out().wait_recv()
        pl.semaphore_wait(go_sem, 1)
        ring_start(relay_hop)
        ring_middle(relay_hop, push_both)
        ring_start(in_hop)
        ring_end(relay_hop)
        push(NZ // 2).start()
        ring_middle(in_hop)
        ring_start(out_hop)
        ring_end(in_hop)
        ring_middle(out_hop)
        ring_end(out_hop)

    def block(ahead):
        return pl.ds(pl.multiple_of((x + ahead) % NX * LEN, LEN), LEN)

    def order(i):
        return i + i // 2 - i // 3 * 2

    def onward(m, ahead, dy):
        return remote(
            h_next.at[m, block(ahead), :],
            act.at[m, y, block(ahead), :],
            next_send.at[m, ahead, dy],
            next_recv.at[m, ahead, dy],
            at(1 - section, z, x, (y + dy) % NY),
        )

    def send_part(m, ahead):
        return remote(
            part.at[m, block(ahead), :],
            got.at[m, ahead],
            part_send.at[m, ahead],
            part_recv.at[m, ahead],
            at(section, z, (x + ahead) % NX, y),
        )

    def send_y(m, ahead):
        return remote(
            y_all.at[m, x],
            y_all.at[m, x],
            y_send.at[m, ahead],
            y_recv.at[m, ahead],
            at(section, z, (x + ahead) % NX, y),
        )

    def send_proj(m, ahead, dy):
        to_y = (y + dy) % NY
        return remote(
            proj.at[m, to_y, block(ahead), :],
            proj_got.at[m, dy, block(ahead), :],
            proj_send.at[m, ahead, dy],
            proj_recv.at[m, ahead, dy],
            at(section, z, x, to_y),
        )

    def send_out(m, ahead, half):
        return remote(
            h_next.at[m, block(ahead), pl.ds(half * LEN, LEN)],
            out_ref.at[0, m, 0, :, pl.ds(pl.multiple_of((x + NX * half) * LEN, LEN), LEN)],
            out_send.at[m, ahead, half],
            out_recv.at[m, ahead, half],
            at(section, z, (x + ahead) % NX, y),
        )

    lane = lax.broadcasted_iota(jnp.int32, (LEN, LEN), 1)
    row = lax.broadcasted_iota(jnp.int32, (LEN, LEN), 0)

    def prepare(m, ahead):
        def scale(i, carry):
            rows = pl.ds(pl.multiple_of((x + ahead) % NX * LEN + i * 64, 64), 64)
            total = jnp.zeros((64, LEN), F32)
            for yy in range(NY):
                for half in range(2):
                    at_ = yy * 2 * LEN + half * LEN
                    value = act[m, yy, rows, half * LEN : (half + 1) * LEN].astype(F32)
                    total = total + value * value
                    gain = gains[
                        :, pl.ds(pl.multiple_of((yy * 2 + half) * NX * LEN + x * LEN, LEN), LEN)
                    ]
                    scaled[m, rows, at_ : at_ + LEN] = (value * gain).astype(BF16)
            squares[m, rows, :] = jnp.broadcast_to(
                jnp.sum(total, axis=1, keepdims=True), (64, LEN)
            )
            return carry

        lax.fori_loop(0, LEN // 64, scale, 0)

    def project_in(m, ahead):
        rows = block(ahead)
        values = scaled[m, rows, :]
        for c in range((WIDTH + BC) // 256):
            cols = slice(c * 256, (c + 1) * 256)
            part[m, rows, cols] = jnp.dot(
                values, w_in[:, cols], preferred_element_type=F32
            ).astype(BF16)
        small = jnp.dot(values, w_in[:, WIDTH + BC :], preferred_element_type=F32)
        high = small.astype(BF16).astype(F32)
        low = small - high
        square = squares[m, rows, :]
        square_high = square.astype(BF16).astype(F32)
        packed = high + pltpu.roll(low, 16, 1)
        packed = jnp.where(lane == 32, square_high, packed)
        packed = jnp.where(lane == 33, square - square_high, packed)
        part[m, rows, WIDTH + BC :] = packed.astype(BF16)

        @pl.when(ahead != 0)
        def _():
            send_part(m, ahead).start()

    def mix(m):
        for ahead in (1, 3, 2):
            send_part(m, ahead).wait_recv()
        own = block(0)

        def summed(cols):
            total = part[m, own, cols].astype(F32)
            for dx in (1, 2, 3):
                total = total + got[m, dx, :, cols].astype(F32)
            return total

        tail = summed(slice(WIDTH + BC, COLS))
        square = tail[:, 32:33] + tail[:, 33:34]
        inverse = lax.rsqrt(square * (1.0 / (NX * WIDTH)) + EPS)
        raw = (tail + pltpu.roll(tail, LEN - 16, 1)) * inverse
        pre = raw + jnp.concatenate([biases[...], jnp.zeros((1, LEN - 16), F32)], axis=1)
        steps = jnp.maximum(pre, 0.0) + jnp.log1p(jnp.exp(-jnp.abs(pre)))
        steps = jnp.where(lane < 16, steps, 0.0)
        lower = jnp.where(row >= lane, 1.0, 0.0)
        decay = jnp.dot(
            lower,
            steps * jnp.concatenate([rates[...], jnp.zeros((1, LEN - 16), F32)], axis=1),
            precision=lax.Precision.HIGHEST,
            preferred_element_type=F32,
        )
        decay_t = decay.T
        inverse_wide = jnp.broadcast_to(inverse, (LEN, LEN))

        padded[0:8, :] = jnp.zeros((8, LEN), F32)

        for c in range((WIDTH + BC) // LEN):
            cols = slice(c * LEN, (c + 1) * LEN)
            padded[8:, :] = summed(cols) * inverse_wide
            value = jnp.zeros((LEN, LEN), F32)
            for tap in range(4):
                value = value + taps[tap : tap + 1, cols] * padded[5 + tap : 5 + tap + LEN, :]
            conv[:, cols] = value / (1.0 + jnp.exp(-value))

        scores = lax.dot_general(
            conv[:, WIDTH + STATE : WIDTH + BC],
            conv[:, WIDTH : WIDTH + STATE],
            (((1,), (1,)), ((), ())),
            precision=lax.Precision.HIGHEST,
            preferred_element_type=F32,
        )
        scores = jnp.where(row >= lane, scores, 0.0)
        power = jnp.zeros((LEN, LEN), F32)
        for pair in range(WIDTH // LEN):
            cols = slice(pair * LEN, (pair + 1) * LEN)
            mixes = []
            for j in (2 * pair, 2 * pair + 1):
                gap = jnp.minimum(decay_t[j : j + 1, :] - decay[:, j : j + 1], 0.0)
                mixes.append((jnp.exp(gap) * scores).astype(BF16))
            value = conv[:, cols]
            step = jnp.where(
                lane < HEAD_DIM,
                steps[:, 2 * pair : 2 * pair + 1],
                steps[:, 2 * pair + 1 : 2 * pair + 2],
            )
            stepped = value * step
            blocks = jnp.concatenate(
                [
                    jnp.where(lane < HEAD_DIM, stepped, 0.0).astype(BF16),
                    jnp.where(lane < HEAD_DIM, 0.0, stepped).astype(BF16),
                ],
                axis=0,
            )
            mixed = jnp.dot(
                jnp.concatenate(mixes, axis=1), blocks, preferred_element_type=F32
            )
            skip = jnp.where(
                lane[:1] < HEAD_DIM,
                skips[:, 2 * pair : 2 * pair + 1],
                skips[:, 2 * pair + 1 : 2 * pair + 2],
            )
            mixed = mixed + skip * value
            power = power + mixed * mixed
            y_raw[:, cols] = mixed
        norm = lax.rsqrt(jnp.sum(power, axis=1, keepdims=True) * (1.0 / WIDTH) + EPS)
        norm = jnp.broadcast_to(norm, (LEN, LEN))
        for c in range(WIDTH // LEN):
            cols = slice(c * LEN, (c + 1) * LEN)
            y_all[m, x, :, cols] = (y_raw[:, cols] * norm * y_gains[:, cols]).astype(BF16)
        for ahead in (1, 3, 2):
            send_y(m, ahead).start()

    def project_out(m, ahead):
        values = y_all[m, (x + ahead) % NX]
        for dy in (1, 3, 2, 0):
            to_y = (y + dy) % NY
            cols = pl.ds(pl.multiple_of(to_y * 2 * LEN, 2 * LEN), 2 * LEN)
            proj[m, to_y, block(ahead), :] = jnp.dot(
                values, w_out[:, cols], preferred_element_type=F32
            ).astype(BF16)
            if dy:
                send_proj(m, ahead, dy).start()

    def finish(m, ahead):
        for dy in (1, 3, 2):
            send_proj(m, ahead, dy).wait_recv()
        rows = block(ahead)
        total = proj[m, y, rows, :].astype(F32)
        for dy in (1, 2, 3):
            total = total + proj_got[m, dy, rows, :].astype(F32)
        h_next[m, rows, :] = (act[m, y, rows, :].astype(F32) + total).astype(BF16)

        @pl.when(section == 0)
        def _():
            for dy in (1, 3, 2, 0):
                onward(m, ahead, dy).start()

        @pl.when(ahead != 0)
        def _():
            for half in range(2):
                send_out(m, ahead, half).start()

        @pl.when(ahead == 0)
        def _():
            for half in range(2):
                out_ref[
                    0, m, 0, :, pl.ds(pl.multiple_of((x + NX * half) * LEN, LEN), LEN)
                ] = h_next[m, rows, half * LEN : (half + 1) * LEN]

    @pl.when(section == 0)
    def _():
        for m in range(MICRO):
            for dx in range(NX):
                for dy in range(NY):
                    if dx or dy:
                        first(m, dx, dy).wait_recv()

        def all_rows(i, carry):
            prepare(i // NX, i % NX)
            return carry

        lax.fori_loop(0, MICRO * NX, all_rows, 0)
        ring_end(in_hop)

    def stage_in(i, carry):
        m = i // NX
        ahead = order((i + 1 - section) % NX)

        @pl.when(section == 1)
        def _():
            for dy in range(NY):
                onward(m, ahead, dy).wait_recv()
            prepare(m, ahead)

        project_in(m, ahead)
        return carry

    lax.fori_loop(0, MICRO * NX, stage_in, 0)

    @pl.when(section == 0)
    def _():
        for step in range(1, NZ):
            push(step).wait_recv()

    def stage_mix(m, carry):
        mix(m)
        project_out(m, 0)
        finish(m, 0)
        return carry

    lax.fori_loop(0, MICRO, stage_mix, 0)

    def stage_out(i, carry):
        @pl.when(i < MICRO * (NX - 1))
        def _():
            m = i // (NX - 1)
            ahead = order(i % (NX - 1) + 1)
            send_y(m, (NX - ahead) % NX).wait_recv()
            project_out(m, ahead)

        @pl.when(i > 0)
        def _():
            finish((i - 1) // (NX - 1), order((i - 1) % (NX - 1) + 1))

        return carry

    lax.fori_loop(0, MICRO * (NX - 1) + 1, stage_out, 0)

    def drain(m, carry):
        for ahead in (1, 2, 3):
            for half in range(2):
                send_out(m, ahead, half).wait()
            send_part(m, ahead).wait_send()
            send_y(m, ahead).wait_send()
        for ahead in range(NX):
            for dy in (1, 2, 3):
                send_proj(m, ahead, dy).wait_send()

        @pl.when(section == 0)
        def _():
            for ahead in range(NX):
                for dy in range(NY):
                    onward(m, ahead, dy).wait_send()
                    if ahead or dy:
                        first(m, ahead, dy).wait_send()

        return carry

    lax.fori_loop(0, MICRO, drain, 0)
    ring_drain(in_hop)

    @pl.when(section == 0)
    def _():
        own_out().wait_send()

    @pl.when(section == 1)
    def _():
        ring_drain(relay_hop)
        ring_drain(out_hop)
        for step in range(1, NZ):
            push(step).wait_send()


def body(
    stream, norm_gain, w_x, w_bc, w_dt, conv_x, conv_bc, dt_bias, decay_rate, skip_d, y_gain, w_out
):
    vmem = pl.BlockSpec(memory_space=pltpu.VMEM)
    whole = pl.BlockSpec(memory_space=pltpu.HBM)
    dma = pltpu.SemaphoreType.DMA
    return pl.pallas_call(
        kernel,
        out_shape=jax.ShapeDtypeStruct((1, MICRO, 1, LEN, WIDTH), BF16),
        in_specs=[whole] * 12,
        out_specs=vmem,
        scratch_shapes=[
            pltpu.VMEM((MICRO, NX, LEN, 2 * LEN), BF16),
            pltpu.VMEM((1, NX * WIDTH), F32),
            pltpu.VMEM((LEN, 16), BF16),
            pltpu.VMEM((4, WIDTH + BC), F32),
            pltpu.VMEM((1, 16), F32),
            pltpu.VMEM((1, 16), F32),
            pltpu.VMEM((1, 16), F32),
            pltpu.VMEM((1, WIDTH), F32),
            pltpu.VMEM((NZ * LEN, COLS), BF16),
            pltpu.VMEM((WIDTH, NZ * LEN), BF16),
            pltpu.VMEM((WIDTH, NZ * LEN), BF16),
            pltpu.VMEM((MICRO, NY, ROWS, 2 * LEN), BF16),
            pltpu.VMEM((MICRO, ROWS, WIDTH), BF16),
            pltpu.VMEM((MICRO, ROWS, COLS), BF16),
            pltpu.VMEM((MICRO, NX, LEN, COLS), BF16),
            pltpu.VMEM((8 + LEN, LEN), F32),
            pltpu.VMEM((LEN, WIDTH + BC), F32),
            pltpu.VMEM((LEN, WIDTH), F32),
            pltpu.VMEM((MICRO, NX, LEN, WIDTH), BF16),
            pltpu.VMEM((MICRO, NY, ROWS, 2 * LEN), BF16),
            pltpu.VMEM((MICRO, NY, ROWS, 2 * LEN), BF16),
            pltpu.VMEM((MICRO, ROWS, 2 * LEN), BF16),
            pltpu.VMEM((MICRO, ROWS, LEN), F32),
            dma((2, 4, CHUNKS)),
            dma((2, 4, CHUNKS)),
            dma((2, 4, CHUNKS)),
            dma((2, 4, CHUNKS)),
            dma((MICRO, NX, NY)),
            dma((MICRO, NX, NY)),
            dma((MICRO, NX, NY)),
            dma((MICRO, NX, NY)),
            dma((MICRO, NX)),
            dma((MICRO, NX)),
            dma((MICRO, NX)),
            dma((MICRO, NX)),
            dma((MICRO, NX, NY)),
            dma((MICRO, NX, NY)),
            dma((MICRO, NX, 2)),
            dma((MICRO, NX, 2)),
            dma((2, 4, CHUNKS)),
            dma((2, 4, CHUNKS)),
            dma((NZ,)),
            dma((NZ,)),
            dma,
            dma,
            dma((11,)),
            dma((MICRO, NX, 2)),
            pltpu.SemaphoreType.REGULAR,
        ],
        compiler_params=pltpu.CompilerParams(
            collective_id=0, has_side_effects=True, vmem_limit_bytes=60 * 1024 * 1024
        ),
        name="mixer",
    )(
        stream,
        norm_gain,
        w_x,
        w_bc,
        w_dt,
        conv_x,
        conv_bc,
        dt_bias,
        decay_rate,
        skip_d,
        y_gain,
        w_out,
    )


def solution(mesh):
    in_specs = (
        P(None, "dp", None, "head"),
        P("section", None),
        P("section", "dp", "head"),
        P("section", "dp", "head"),
        P("section", "dp", "head"),
        P("section", None, "head"),
        P("section", None, "head"),
        P("section", "head"),
        P("section", "head"),
        P("section", "head"),
        P("section", "head"),
        P("section", "head", "dp"),
    )
    out_specs = P("section", None, "dp", None, "head")
    return jax.shard_map(body, mesh=mesh, in_specs=in_specs, out_specs=out_specs, check_vma=False)
```

time: 146 us -> 122 us (0.84)
  Pallas kernels: 140 us -> 119 us
  local copies, waits for them, and re-layouts: 5.96 us -> 3.27 us
    pallas_call x1, Pallas kernels: 140 us -> 119 us  [body(): pl.pallas_call(kernel, out_shape=jax.ShapeDtypeStruct((1, MICRO, 1, LEN,...]
    unnamed x27 -> x2, local copies, waits for them, and re-layouts: 5.66 us -> 3.27 us
where the time goes in v2:
time: 122 us
  Pallas kernels  119 us (98%)
  local copies, waits for them, and re-layouts  3.27 us (3%)
    pallas_call x1, Pallas kernels, body(): pl.pallas_call(kernel, out_shape=jax.ShapeDtypeStruct((1, MICRO, 1, LEN,...  119 us
    unnamed x2, local copies, waits for them, and re-layouts  3.27 us

profile of v2, /device:TPU:1, one launch (start us, length us, event | category | flops | bytes accessed | tf_op | source)
XLA Modules:
  0.0 122.3 jit_solution(17226209389214488023)
XLA Ops:
  0.0 1.4 %copy.13.w_dt_ref = bf16[1,128,16]{2,1,0:T(8,128)(2,1)} copy(bf16[1,128,16]{1,2,0:T(8,128)(2,1)} %param.16) | data formatting | bytes 8192 | tf_op args[4]
  1.4 119.0 %mixer.1 = bf16[1,2,1,128,1024]{4,3,2,1,0:T(8,128)(2,1)} custom-call(bf16[2,1,128,1024]{3,2,1,0:T(8,128)(2,1)} %stream_ref.1, f32[1,4096]{1,0:T(1,128)} %gain_ref.1, bf16[1,128,1024]{2,1,0:T(8,128)(2,1)} %w_x_ref.1, bf16[1,128,256]{2,1,0:T(8,128)(2,1)} %w_bc_ref.1, bf16[1,128,16]{2,1,0:T(8,128)(2,1)} %copy.13.w_dt_ref, f32[1,4,1024]{2,1,0:T(4,128)} %conv_x_ref.1, ...), custom_call_target="tpu_custom_call" | custom-call | tf_op jit(solution)/shard_map/mixer/pallas_call | solution.py:618
  120.4 1.9 %copy.15 = bf16[1,2,1,128,1024]{4,3,2,1,0:T(8,128)(2,1)} copy(bf16[1,2,1,128,1024]{4,3,2,1,0:T(8,128)(2,1)} %mixer.1) | data formatting | bytes 1048576

commit v3 on v2

--- a/solution.py
+++ b/solution.py
@@ -20,6 +20,7 @@
 BC = 2 * STATE
 COLS = WIDTH + BC + 128
 CHUNKS = 4
+HALF = LEN // 2
 EPS = 1e-05
 F32 = jnp.float32
 BF16 = jnp.bfloat16
@@ -52,7 +53,6 @@
     out_ref,
     staged,
     gains,
-    w_dt,
     taps,
     biases,
     rates,
@@ -61,10 +61,12 @@
     w_in,
     w_out,
     relay,
+    w_step,
     act,
     scaled,
     part,
     got,
+    hop_got,
     padded,
     conv,
     y_raw,
@@ -75,16 +77,22 @@
     squares,
     in_send,
     in_recv,
+    step_send,
+    step_recv,
     wout_send,
     wout_recv,
     first_send,
     first_recv,
     next_send,
     next_recv,
+    hop_send,
+    hop_recv,
     part_send,
     part_recv,
     y_send,
     y_recv,
+    pass_send,
+    pass_recv,
     proj_send,
     proj_recv,
     out_send,
@@ -119,7 +127,7 @@
                 (w_out_ref.at[0], w_out.at[:, own_block]),
                 (w_x_ref.at[0], w_in.at[own_block, :WIDTH]),
                 (w_bc_ref.at[0], w_in.at[own_block, WIDTH : WIDTH + BC]),
-                (w_dt_ref.at[0], w_dt),
+                (w_dt_ref.at[0], w_step.at[:16, own_block]),
                 (gain_ref, gains),
                 (conv_x_ref.at[0], taps.at[:, :WIDTH]),
                 (conv_bc_ref.at[0], taps.at[:, WIDTH:]),
@@ -188,6 +196,17 @@
 
         return one
 
+    def step_hop(direction, step):
+        owner = (z + NZ - step) % NZ if direction == 0 else (z + step) % NZ
+        piece = w_step.at[:16, pl.ds(pl.multiple_of(owner * LEN, LEN), LEN)]
+        return remote(
+            piece,
+            piece,
+            step_send.at[direction, step],
+            step_recv.at[direction, step],
+            at(section, right if direction == 0 else left, x, y),
+        )
+
     in_hop = hop(w_in, True, in_send, in_recv)
     out_hop = hop(w_out, False, wout_send, wout_recv)
     relay_hop = hop(relay, False, relay_send, relay_recv)
@@ -202,24 +221,40 @@
         ]
 
     def ring_start(one):
+        if one is in_hop:
+            for direction in range(2):
+                step_hop(direction, 0).start()
         for chunk, direction in pieces(0):
             one(direction, 0, chunk).start()
 
+    def ring_step(one, step):
+        if one is in_hop:
+            for direction in range(2):
+                step_hop(direction, step - 1).wait_recv()
+                if step < 3 or direction == 0:
+                    step_hop(direction, step).start()
+        for chunk, direction in pieces(0):
+            one(direction, step - 1, chunk).wait_recv()
+            if (chunk, direction) in pieces(step):
+                one(direction, step, chunk).start()
+
     def ring_middle(one, arrived=None):
         for step in range(1, 4):
-            for chunk, direction in pieces(0):
-                one(direction, step - 1, chunk).wait_recv()
-                if (chunk, direction) in pieces(step):
-                    one(direction, step, chunk).start()
+            ring_step(one, step)
             if arrived is not None:
                 arrived(step)
 
     def ring_end(one):
+        if one is in_hop:
+            step_hop(0, 3).wait_recv()
         for chunk, direction in pieces(3):
             one(direction, 3, chunk).wait_recv()
 
     def ring_drain(one):
         for step in range(4):
+            if one is in_hop:
+                for direction in range(2 if step < 3 else 1):
+                    step_hop(direction, step).wait_send()
             for chunk, direction in pieces(step):
                 one(direction, step, chunk).wait_send()
 
@@ -250,10 +285,7 @@
 
     for load in loads[1:]:
         load.wait()
-    w_in[own_block, WIDTH + BC :] = jnp.concatenate(
-        [w_dt[...], jnp.zeros((LEN, LEN - 16), BF16)], axis=1
-    )
-
+    w_step[16:, :] = jnp.zeros((LEN - 16, NZ * LEN), BF16)
     def first(m, dx, dy):
         to_x = (x + dx) % NX
         to_y = (y + dy) % NY
@@ -292,8 +324,6 @@
         ring_middle(in_hop)
         ring_start(out_hop)
         ring_end(in_hop)
-        ring_middle(out_hop)
-        ring_end(out_hop)
 
     def block(ahead):
         return pl.ds(pl.multiple_of((x + ahead) % NX * LEN, LEN), LEN)
@@ -310,23 +340,79 @@
             at(1 - section, z, x, (y + dy) % NY),
         )
 
-    def send_part(m, ahead):
-        return remote(
-            part.at[m, block(ahead), :],
-            got.at[m, ahead],
-            part_send.at[m, ahead],
-            part_recv.at[m, ahead],
-            at(section, z, (x + ahead) % NX, y),
-        )
-
-    def send_y(m, ahead):
-        return remote(
-            y_all.at[m, x],
-            y_all.at[m, x],
-            y_send.at[m, ahead],
-            y_recv.at[m, ahead],
-            at(section, z, (x + ahead) % NX, y),
-        )
+    def towards(direction):
+        return at(section, z, (x + 1 + 2 * direction) % NX, y)
+
+    def half_block(ahead, half):
+        return pl.ds(pl.multiple_of((x + ahead) % NX * LEN + half * HALF, HALF), HALF)
+
+    def send_hop(m, direction):
+        return remote(
+            part.at[m, half_block(2, direction), :],
+            hop_got.at[m, direction],
+            hop_send.at[m, direction],
+            hop_recv.at[m, direction],
+            towards(direction),
+        )
+
+    def send_part(m, direction, half):
+        return remote(
+            part.at[m, half_block(1 + 2 * direction, half), :],
+            got.at[m, direction, pl.ds(half * HALF, HALF), :],
+            part_send.at[m, direction, half],
+            part_recv.at[m, direction, half],
+            towards(direction),
+        )
+
+    def fold(m):
+        for direction in range(2):
+            send_hop(m, direction).wait_recv()
+            rows = half_block(1 + 2 * direction, direction)
+            for c in range(COLS // LEN):
+                cols = slice(c * LEN, (c + 1) * LEN)
+                part[m, rows, cols] = (
+                    part[m, rows, cols].astype(F32) + hop_got[m, direction, :, cols].astype(F32)
+                ).astype(BF16)
+            send_part(m, direction, direction).start()
+
+    def send_y(m, direction, half):
+        piece = y_all.at[m, x, pl.ds(half * HALF, HALF), :]
+        return remote(
+            piece,
+            piece,
+            y_send.at[m, direction, half],
+            y_recv.at[m, direction, half],
+            towards(direction),
+        )
+
+    def pass_y(m, direction):
+        piece = y_all.at[m, (x + 3 - 2 * direction) % NX, pl.ds(direction * HALF, HALF), :]
+        return remote(
+            piece,
+            piece,
+            pass_send.at[m, direction],
+            pass_recv.at[m, direction],
+            towards(direction),
+        )
+
+    def pass_on(m):
+        for direction in range(2):
+            send_y(m, direction, direction).wait_recv()
+            pass_y(m, direction).start()
+
+    def wait_y(m, ahead):
+        @pl.when(ahead == 1)
+        def _():
+            send_y(m, 1, 0).wait_recv()
+
+        @pl.when(ahead == 3)
+        def _():
+            send_y(m, 0, 1).wait_recv()
+
+        @pl.when(ahead == 2)
+        def _():
+            for direction in range(2):
+                pass_y(m, direction).wait_recv()
 
     def send_proj(m, ahead, dy):
         to_y = (y + dy) % NY
@@ -378,7 +464,9 @@
             part[m, rows, cols] = jnp.dot(
                 values, w_in[:, cols], preferred_element_type=F32
             ).astype(BF16)
-        small = jnp.dot(values, w_in[:, WIDTH + BC :], preferred_element_type=F32)
+        small = lax.dot_general(
+            values, w_step[...], (((1,), (1,)), ((), ())), preferred_element_type=F32
+        )
         high = small.astype(BF16).astype(F32)
         low = small - high
         square = squares[m, rows, :]
@@ -388,19 +476,27 @@
         packed = jnp.where(lane == 33, square - square_high, packed)
         part[m, rows, WIDTH + BC :] = packed.astype(BF16)
 
-        @pl.when(ahead != 0)
-        def _():
-            send_part(m, ahead).start()
+        @pl.when(ahead == 2)
+        def _():
+            for direction in range(2):
+                send_hop(m, direction).start()
+
+        for direction in range(2):
+
+            @pl.when(ahead == 1 + 2 * direction)
+            def _(direction=direction):
+                send_part(m, direction, 1 - direction).start()
 
     def mix(m):
-        for ahead in (1, 3, 2):
-            send_part(m, ahead).wait_recv()
+        for half in range(2):
+            for direction in range(2):
+                send_part(m, direction, half).wait_recv()
         own = block(0)
 
         def summed(cols):
             total = part[m, own, cols].astype(F32)
-            for dx in (1, 2, 3):
-                total = total + got[m, dx, :, cols].astype(F32)
+            for direction in range(2):
+                total = total + got[m, direction, :, cols].astype(F32)
             return total
 
         tail = summed(slice(WIDTH + BC, COLS))
@@ -475,8 +571,9 @@
         for c in range(WIDTH // LEN):
             cols = slice(c * LEN, (c + 1) * LEN)
             y_all[m, x, :, cols] = (y_raw[:, cols] * norm * y_gains[:, cols]).astype(BF16)
-        for ahead in (1, 3, 2):
-            send_y(m, ahead).start()
+        for half in range(2):
+            for direction in range(2):
+                send_y(m, direction, (direction + half) % 2).start()
 
     def project_out(m, ahead):
         values = y_all[m, (x + ahead) % NX]
@@ -489,6 +586,21 @@
             if dy:
                 send_proj(m, ahead, dy).start()
 
+    def give(m, ahead):
+        rows = block(ahead)
+
+        @pl.when(ahead != 0)
+        def _():
+            for half in range(2):
+                send_out(m, ahead, half).start()
+
+        @pl.when(ahead == 0)
+        def _():
+            for half in range(2):
+                out_ref[
+                    0, m, 0, :, pl.ds(pl.multiple_of((x + NX * half) * LEN, LEN), LEN)
+                ] = h_next[m, rows, half * LEN : (half + 1) * LEN]
+
     def finish(m, ahead):
         for dy in (1, 3, 2):
             send_proj(m, ahead, dy).wait_recv()
@@ -503,17 +615,7 @@
             for dy in (1, 3, 2, 0):
                 onward(m, ahead, dy).start()
 
-        @pl.when(ahead != 0)
-        def _():
-            for half in range(2):
-                send_out(m, ahead, half).start()
-
-        @pl.when(ahead == 0)
-        def _():
-            for half in range(2):
-                out_ref[
-                    0, m, 0, :, pl.ds(pl.multiple_of((x + NX * half) * LEN, LEN), LEN)
-                ] = h_next[m, rows, half * LEN : (half + 1) * LEN]
+        pl.when(section == 1)(lambda: give(m, ahead))
 
     @pl.when(section == 0)
     def _():
@@ -530,9 +632,10 @@
         lax.fori_loop(0, MICRO * NX, all_rows, 0)
         ring_end(in_hop)
 
-    def stage_in(i, carry):
+    def rows_in(i, carry):
         m = i // NX
-        ahead = order((i + 1 - section) % NX)
+        turn = i % NX
+        ahead = order(jnp.where(section == 0, NX - 1 - turn, turn))
 
         @pl.when(section == 1)
         def _():
@@ -543,43 +646,80 @@
         project_in(m, ahead)
         return carry
 
-    lax.fori_loop(0, MICRO * NX, stage_in, 0)
+    def second(work):
+        pl.when(section == 1)(work)
+
+    lax.fori_loop(0, NX, rows_in, 0)
+    second(lambda: ring_step(out_hop, 1))
+    lax.fori_loop(NX, NX + 1, rows_in, 0)
+    fold(0)
+    second(lambda: ring_step(out_hop, 2))
+    lax.fori_loop(NX + 1, MICRO * NX, rows_in, 0)
+    second(lambda: ring_step(out_hop, 3))
+    pl.when(section == 0)(lambda: fold(1))
+
+    def stage_mix(m, carry):
+        mix(m)
+
+        @pl.when(m == 0)
+        def _():
+            @pl.when(section == 0)
+            def _():
+                for step in range(1, NZ):
+                    push(step).wait_recv()
+
+            @pl.when(section == 1)
+            def _():
+                fold(1)
+                ring_end(out_hop)
+
+        project_out(m, 0)
+        pl.when(jnp.where(section == 0, m == 1, m == 0))(lambda: pass_on(0))
+        return carry
+
+    lax.fori_loop(0, MICRO, stage_mix, 0)
+    finish(0, 0)
+
+    def stage_end(i, carry):
+        behind = jnp.maximum(i - 1, 0)
+        finish(
+            jnp.where(i == 0, 1, behind // (NX - 1)),
+            jnp.where(i == 0, 0, order(behind % (NX - 1) + 1)),
+        )
+        return carry
+
+    def ended(i):
+        return jnp.where(i < 2, 0, jnp.where(i < 4, 3, jnp.where(i < 5, 4, 7)))
+
+    def stage_out(i, carry):
+        m = i // (NX - 1)
+        ahead = order(i % (NX - 1) + 1)
+        wait_y(m, ahead)
+        project_out(m, ahead)
+        pl.when(i == NX - 2)(lambda: pass_on(1))
+        lax.fori_loop(ended(i - 1), ended(i), stage_end, 0)
+        return carry
+
+    lax.fori_loop(0, MICRO * (NX - 1), stage_out, 0)
 
     @pl.when(section == 0)
     def _():
-        for step in range(1, NZ):
-            push(step).wait_recv()
-
-    def stage_mix(m, carry):
-        mix(m)
-        project_out(m, 0)
-        finish(m, 0)
-        return carry
-
-    lax.fori_loop(0, MICRO, stage_mix, 0)
-
-    def stage_out(i, carry):
-        @pl.when(i < MICRO * (NX - 1))
-        def _():
-            m = i // (NX - 1)
-            ahead = order(i % (NX - 1) + 1)
-            send_y(m, (NX - ahead) % NX).wait_recv()
-            project_out(m, ahead)
-
-        @pl.when(i > 0)
-        def _():
-            finish((i - 1) // (NX - 1), order((i - 1) % (NX - 1) + 1))
-
-        return carry
-
-    lax.fori_loop(0, MICRO * (NX - 1) + 1, stage_out, 0)
+        def later(i, carry):
+            give(i // NX, i % NX)
+            return carry
+
+        lax.fori_loop(0, MICRO * NX, later, 0)
 
     def drain(m, carry):
         for ahead in (1, 2, 3):
             for half in range(2):
                 send_out(m, ahead, half).wait()
-            send_part(m, ahead).wait_send()
-            send_y(m, ahead).wait_send()
+        for direction in range(2):
+            for half in range(2):
+                send_part(m, direction, half).wait_send()
+                send_y(m, direction, half).wait_send()
+            send_hop(m, direction).wait_send()
+            pass_y(m, direction).wait_send()
         for ahead in range(NX):
             for dy in (1, 2, 3):
                 send_proj(m, ahead, dy).wait_send()
@@ -623,19 +763,20 @@
         scratch_shapes=[
             pltpu.VMEM((MICRO, NX, LEN, 2 * LEN), BF16),
             pltpu.VMEM((1, NX * WIDTH), F32),
-            pltpu.VMEM((LEN, 16), BF16),
             pltpu.VMEM((4, WIDTH + BC), F32),
             pltpu.VMEM((1, 16), F32),
             pltpu.VMEM((1, 16), F32),
             pltpu.VMEM((1, 16), F32),
             pltpu.VMEM((1, WIDTH), F32),
-            pltpu.VMEM((NZ * LEN, COLS), BF16),
+            pltpu.VMEM((NZ * LEN, WIDTH + BC), BF16),
             pltpu.VMEM((WIDTH, NZ * LEN), BF16),
             pltpu.VMEM((WIDTH, NZ * LEN), BF16),
+            pltpu.VMEM((LEN, NZ * LEN), BF16),
             pltpu.VMEM((MICRO, NY, ROWS, 2 * LEN), BF16),
             pltpu.VMEM((MICRO, ROWS, WIDTH), BF16),
             pltpu.VMEM((MICRO, ROWS, COLS), BF16),
-            pltpu.VMEM((MICRO, NX, LEN, COLS), BF16),
+            pltpu.VMEM((MICRO, 2, LEN, COLS), BF16),
+            pltpu.VMEM((MICRO, 2, HALF, COLS), BF16),
             pltpu.VMEM((8 + LEN, LEN), F32),
             pltpu.VMEM((LEN, WIDTH + BC), F32),
             pltpu.VMEM((LEN, WIDTH), F32),
@@ -646,16 +787,22 @@
             pltpu.VMEM((MICRO, ROWS, LEN), F32),
             dma((2, 4, CHUNKS)),
             dma((2, 4, CHUNKS)),
+            dma((2, 4)),
+            dma((2, 4)),
             dma((2, 4, CHUNKS)),
             dma((2, 4, CHUNKS)),
             dma((MICRO, NX, NY)),
             dma((MICRO, NX, NY)),
             dma((MICRO, NX, NY)),
             dma((MICRO, NX, NY)),
-            dma((MICRO, NX)),
-            dma((MICRO, NX)),
-            dma((MICRO, NX)),
-            dma((MICRO, NX)),
+            dma((MICRO, 2)),
+            dma((MICRO, 2)),
+            dma((MICRO, 2, 2)),
+            dma((MICRO, 2, 2)),
+            dma((MICRO, 2, 2)),
+            dma((MICRO, 2, 2)),
+            dma((MICRO, 2)),
+            dma((MICRO, 2)),
             dma((MICRO, NX, NY)),
             dma((MICRO, NX, NY)),
             dma((MICRO, NX, 2)),
@@ -679,7 +826,7 @@
         norm_gain,
         w_x,
         w_bc,
-        w_dt,
+        jnp.swapaxes(w_dt, 1, 2),
         conv_x,
         conv_bc,
         dt_bias,

time: 122 us -> 115 us (0.943)
  Pallas kernels: 119 us -> 113 us
  local copies, waits for them, and re-layouts: 3.27 us -> 1.87 us
    pallas_call x1, Pallas kernels: 119 us -> 113 us  [body(): pl.pallas_call(kernel, out_shape=jax.ShapeDtypeStruct((1, MICRO, 1, LEN,...]
    unnamed x2 -> x1, local copies, waits for them, and re-layouts: 3.27 us -> 1.87 us
where the time goes in v3:
time: 115 us
  Pallas kernels  113 us (98%)
  local copies, waits for them, and re-layouts  1.87 us (2%)
    pallas_call x1, Pallas kernels, body(): pl.pallas_call(kernel, out_shape=jax.ShapeDtypeStruct((1, MICRO, 1, LEN,...  113 us

profile of v3, /device:TPU:1, one launch (start us, length us, event | category | flops | bytes accessed | tf_op | source)
XLA Modules:
  0.0 114.7 jit_solution(15813217170335333819)
XLA Ops:
  0.0 112.9 %mixer.1 = bf16[1,2,1,128,1024]{4,3,2,1,0:T(8,128)(2,1)} custom-call(bf16[2,1,128,1024]{3,2,1,0:T(8,128)(2,1)} %stream_ref.1, f32[1,4096]{1,0:T(1,128)} %gain_ref.1, bf16[1,128,1024]{2,1,0:T(8,128)(2,1)} %w_x_ref.1, bf16[1,128,256]{2,1,0:T(8,128)(2,1)} %w_bc_ref.1, bf16[1,16,128]{2,1,0:T(8,128)(2,1)} %bitcast.1, f32[1,4,1024]{2,1,0:T(4,128)} %conv_x_ref.1, ...), custom_call_target="tpu_custom_call" | custom-call | tf_op jit(solution)/shard_map/mixer/pallas_call | solution.py:758
  112.9 1.9 %copy.14 = bf16[1,2,1,128,1024]{4,3,2,1,0:T(8,128)(2,1)} copy(bf16[1,2,1,128,1024]{4,3,2,1,0:T(8,128)(2,1)} %mixer.1) | data formatting | bytes 1048576

commit v4 on v3

--- a/solution.py
+++ b/solution.py
@@ -67,6 +67,7 @@
     part,
     got,
     hop_got,
+    far_got,
     padded,
     conv,
     y_raw,
@@ -87,6 +88,8 @@
     next_recv,
     hop_send,
     hop_recv,
+    far_send,
+    far_recv,
     part_send,
     part_recv,
     y_send,
@@ -105,6 +108,7 @@
     own_recv,
     load_sem,
     stream_sem,
+    keep_sem,
     go_sem,
 ):
     section = lax.axis_index("section")
@@ -143,17 +147,19 @@
 
     def stage(m, xx, half):
         return pltpu.make_async_copy(
-            stream_ref.at[m, 0, :, pl.ds((xx + NX * half) * LEN, LEN)],
+            stream_ref.at[m, 0, :, pl.ds(pl.multiple_of((xx + NX * half) * LEN, LEN), LEN)],
             staged.at[m, xx, :, pl.ds(half * LEN, LEN)],
             stream_sem.at[m, xx, half],
         )
 
     @pl.when(section == 0)
     def _():
-        for m in range(MICRO):
-            for xx in range(NX):
-                for half in range(2):
-                    stage(m, xx, half).start()
+        def work(i, carry):
+            for half in range(2):
+                stage(i // NX, i % NX, half).start()
+            return carry
+
+        lax.fori_loop(0, MICRO * NX, work, 0)
 
     barrier = pltpu.get_barrier_semaphore()
     for dx in range(NX):
@@ -211,52 +217,92 @@
     out_hop = hop(w_out, False, wout_send, wout_recv)
     relay_hop = hop(relay, False, relay_send, relay_recv)
 
-    def pieces(step):
-        half = CHUNKS // 2
-        return [
-            (chunk, direction)
-            for chunk in range(CHUNKS)
-            for direction in range(2)
-            if step < 3 or chunk // half == direction
-        ]
+    def loop(count, work):
+        def one(i, carry):
+            work(i)
+            return carry
+
+        lax.fori_loop(0, count, one, 0)
 
     def ring_start(one):
         if one is in_hop:
             for direction in range(2):
                 step_hop(direction, 0).start()
-        for chunk, direction in pieces(0):
-            one(direction, 0, chunk).start()
+
+        def work(chunk):
+            for direction in range(2):
+                one(direction, 0, chunk).start()
+
+        loop(CHUNKS, work)
 
     def ring_step(one, step):
         if one is in_hop:
             for direction in range(2):
                 step_hop(direction, step - 1).wait_recv()
-                if step < 3 or direction == 0:
-                    step_hop(direction, step).start()
-        for chunk, direction in pieces(0):
-            one(direction, step - 1, chunk).wait_recv()
-            if (chunk, direction) in pieces(step):
+                step_hop(direction, step).start()
+
+        def work(chunk):
+            for direction in range(2):
+                one(direction, step - 1, chunk).wait_recv()
                 one(direction, step, chunk).start()
 
+        loop(CHUNKS, work)
+
+    def ring_last(one):
+        if one is in_hop:
+            for direction in range(2):
+                step_hop(direction, 2).wait_recv()
+            step_hop(0, 3).start()
+
+        def work(chunk):
+            for direction in range(2):
+                one(direction, 2, chunk).wait_recv()
+                pl.when(chunk // (CHUNKS // 2) == direction)(
+                    lambda direction=direction: one(direction, 3, chunk).start()
+                )
+
+        loop(CHUNKS, work)
+
     def ring_middle(one, arrived=None):
-        for step in range(1, 4):
-            ring_step(one, step)
+        def work(i):
+            ring_step(one, i + 1)
             if arrived is not None:
-                arrived(step)
+                arrived(i + 1)
+
+        loop(2, work)
+        ring_last(one)
+        if arrived is not None:
+            arrived(3)
 
     def ring_end(one):
         if one is in_hop:
             step_hop(0, 3).wait_recv()
-        for chunk, direction in pieces(3):
-            one(direction, 3, chunk).wait_recv()
+        for direction in range(2):
+            loop(
+                CHUNKS // 2,
+                lambda i, direction=direction: one(
+                    direction, 3, direction * (CHUNKS // 2) + i
+                ).wait_recv(),
+            )
 
     def ring_drain(one):
-        for step in range(4):
-            if one is in_hop:
+        if one is in_hop:
+            for step in range(4):
                 for direction in range(2 if step < 3 else 1):
                     step_hop(direction, step).wait_send()
-            for chunk, direction in pieces(step):
-                one(direction, step, chunk).wait_send()
+
+        def work(i):
+            for direction in range(2):
+                one(direction, i // CHUNKS, i % CHUNKS).wait_send()
+
+        loop(3 * CHUNKS, work)
+        for direction in range(2):
+            loop(
+                CHUNKS // 2,
+                lambda i, direction=direction: one(
+                    direction, 3, direction * (CHUNKS // 2) + i
+                ).wait_send(),
+            )
 
     def own_out():
         return remote(
@@ -297,34 +343,6 @@
             at(0, z, to_x, to_y),
         )
 
-    @pl.when(section == 0)
-    def _():
-        ring_start(in_hop)
-        for m in range(MICRO):
-            for xx in range(NX):
-                for half in range(2):
-                    stage(m, xx, half).wait()
-            act[m, y, pl.ds(pl.multiple_of(x * LEN, LEN), LEN), :] = staged[m, x]
-            for dx in range(NX):
-                for dy in range(NY):
-                    if dx or dy:
-                        first(m, dx, dy).start()
-        ring_middle(in_hop)
-        pl.semaphore_signal(go_sem, inc=1, device_id=sibling, device_id_type=MESH)
-
-    @pl.when(section == 1)
-    def _():
-        own_out().wait_recv()
-        pl.semaphore_wait(go_sem, 1)
-        ring_start(relay_hop)
-        ring_middle(relay_hop, push_both)
-        ring_start(in_hop)
-        ring_end(relay_hop)
-        push(NZ // 2).start()
-        ring_middle(in_hop)
-        ring_start(out_hop)
-        ring_end(in_hop)
-
     def block(ahead):
         return pl.ds(pl.multiple_of((x + ahead) % NX * LEN, LEN), LEN)
 
@@ -353,6 +371,15 @@
             hop_send.at[m, direction],
             hop_recv.at[m, direction],
             towards(direction),
+        )
+
+    def send_far(m):
+        return remote(
+            part.at[m, block(2), :],
+            far_got.at[m],
+            far_send.at[m],
+            far_recv.at[m],
+            at(section, z, (x + 2) % NX, y),
         )
 
     def send_part(m, direction, half):
@@ -478,23 +505,29 @@
 
         @pl.when(ahead == 2)
         def _():
-            for direction in range(2):
-                send_hop(m, direction).start()
+            @pl.when(section == 0)
+            def _():
+                for direction in range(2):
+                    send_hop(m, direction).start()
+
+            pl.when(section == 1)(lambda: send_far(m).start())
 
         for direction in range(2):
 
             @pl.when(ahead == 1 + 2 * direction)
             def _(direction=direction):
                 send_part(m, direction, 1 - direction).start()
+                pl.when(section == 1)(lambda: send_part(m, direction, direction).start())
 
     def mix(m):
         for half in range(2):
             for direction in range(2):
                 send_part(m, direction, half).wait_recv()
+        pl.when(section == 1)(lambda: send_far(m).wait_recv())
         own = block(0)
 
         def summed(cols):
-            total = part[m, own, cols].astype(F32)
+            total = part[m, own, cols].astype(F32) + far_got[m, :, cols].astype(F32)
             for direction in range(2):
                 total = total + got[m, direction, :, cols].astype(F32)
             return total
@@ -586,6 +619,13 @@
             if dy:
                 send_proj(m, ahead, dy).start()
 
+    def keep(m, half):
+        return pltpu.make_async_copy(
+            h_next.at[m, block(0), pl.ds(half * LEN, LEN)],
+            out_ref.at[0, m, 0, :, pl.ds(pl.multiple_of((x + NX * half) * LEN, LEN), LEN)],
+            keep_sem.at[m, half],
+        )
+
     def give(m, ahead):
         rows = block(ahead)
 
@@ -597,9 +637,7 @@
         @pl.when(ahead == 0)
         def _():
             for half in range(2):
-                out_ref[
-                    0, m, 0, :, pl.ds(pl.multiple_of((x + NX * half) * LEN, LEN), LEN)
-                ] = h_next[m, rows, half * LEN : (half + 1) * LEN]
+                keep(m, half).start()
 
     def finish(m, ahead):
         for dy in (1, 3, 2):
@@ -617,20 +655,60 @@
 
         pl.when(section == 1)(lambda: give(m, ahead))
 
+    def plane(work):
+        def one(i, carry):
+            pl.when(i % (NX * NY) != 0)(
+                lambda: work(i // (NX * NY), i // NY % NX, i % NY)
+            )
+            return carry
+
+        lax.fori_loop(0, MICRO * NX * NY, one, 0)
+
+    @pl.when(section == 1)
+    def _():
+        own_out().wait_recv()
+        pl.semaphore_wait(go_sem, 1)
+        ring_start(relay_hop)
+        ring_middle(relay_hop, push_both)
+
+    ring_start(in_hop)
+
     @pl.when(section == 0)
     def _():
+        def arrange(m):
+            def work(xx):
+                for half in range(2):
+                    stage(m, xx, half).wait()
+
+            loop(NX, work)
+            act[m, y, pl.ds(pl.multiple_of(x * LEN, LEN), LEN), :] = staged[m, x]
+
+        loop(MICRO, arrange)
+        plane(lambda m, dx, dy: first(m, dx, dy).start())
         for m in range(MICRO):
-            for dx in range(NX):
-                for dy in range(NY):
-                    if dx or dy:
-                        first(m, dx, dy).wait_recv()
-
-        def all_rows(i, carry):
-            prepare(i // NX, i % NX)
-            return carry
-
-        lax.fori_loop(0, MICRO * NX, all_rows, 0)
-        ring_end(in_hop)
+            far_got[m] = jnp.zeros((LEN, COLS), BF16)
+
+    @pl.when(section == 1)
+    def _():
+        ring_end(relay_hop)
+        push(NZ // 2).start()
+
+    ring_middle(in_hop)
+
+    @pl.when(section == 0)
+    def _():
+        pl.semaphore_signal(go_sem, inc=1, device_id=sibling, device_id_type=MESH)
+        plane(lambda m, dx, dy: first(m, dx, dy).wait_recv())
+        loop(MICRO * NX, lambda i: prepare(i // NX, i % NX))
+
+    @pl.when(section == 1)
+    def _():
+        ring_start(out_hop)
+        ring_drain(relay_hop)
+        loop(NZ - 1, lambda step: push(step + 1).wait_send())
+
+    ring_end(in_hop)
+    pl.when(section == 1)(lambda: ring_drain(in_hop))
 
     def rows_in(i, carry):
         m = i // NX
@@ -646,61 +724,64 @@
         project_in(m, ahead)
         return carry
 
-    def second(work):
-        pl.when(section == 1)(work)
-
-    lax.fori_loop(0, NX, rows_in, 0)
-    second(lambda: ring_step(out_hop, 1))
-    lax.fori_loop(NX, NX + 1, rows_in, 0)
-    fold(0)
-    second(lambda: ring_step(out_hop, 2))
-    lax.fori_loop(NX + 1, MICRO * NX, rows_in, 0)
-    second(lambda: ring_step(out_hop, 3))
-    pl.when(section == 0)(lambda: fold(1))
-
-    def stage_mix(m, carry):
-        mix(m)
-
-        @pl.when(m == 0)
-        def _():
-            @pl.when(section == 0)
+    def rows_and_more(i):
+        rows_in(i, 0)
+        pl.when(jnp.logical_and(section == 0, jnp.logical_or(i == NX, i == MICRO * NX - 1)))(
+            lambda: fold(jnp.where(i == NX, 0, 1))
+        )
+
+        @pl.when(section == 1)
+        def _():
+            pl.when(jnp.logical_or(i == NX - 1, i == NX))(lambda: ring_step(out_hop, i - 2))
+            pl.when(i == MICRO * NX - 1)(lambda: ring_last(out_hop))
+
+    loop(MICRO * NX, rows_and_more)
+
+    def unit(i):
+        behind = jnp.maximum(i - 2, 0)
+        return (
+            jnp.where(i < 2, i, behind // (NX - 1)),
+            jnp.where(i < 2, 0, order(behind % (NX - 1) + 1)),
+        )
+
+    def ended(i):
+        return jnp.where(
+            i < 1, 0, jnp.where(i < 4, 1, jnp.where(i < 6, 4, jnp.where(i < 7, 5, 8)))
+        )
+
+    def stage_out(i):
+        m, ahead = unit(i)
+
+        @pl.when(i < 2)
+        def _():
+            mix(m)
+
+            @pl.when(m == 0)
             def _():
-                for step in range(1, NZ):
-                    push(step).wait_recv()
-
-            @pl.when(section == 1)
-            def _():
-                fold(1)
-                ring_end(out_hop)
-
-        project_out(m, 0)
-        pl.when(jnp.where(section == 0, m == 1, m == 0))(lambda: pass_on(0))
-        return carry
-
-    lax.fori_loop(0, MICRO, stage_mix, 0)
-    finish(0, 0)
-
-    def stage_end(i, carry):
-        behind = jnp.maximum(i - 1, 0)
-        finish(
-            jnp.where(i == 0, 1, behind // (NX - 1)),
-            jnp.where(i == 0, 0, order(behind % (NX - 1) + 1)),
-        )
-        return carry
-
-    def ended(i):
-        return jnp.where(i < 2, 0, jnp.where(i < 4, 3, jnp.where(i < 5, 4, 7)))
-
-    def stage_out(i, carry):
-        m = i // (NX - 1)
-        ahead = order(i % (NX - 1) + 1)
-        wait_y(m, ahead)
+                @pl.when(section == 0)
+                def _():
+                    loop(NZ - 1, lambda step: push(step + 1).wait_recv())
+
+                @pl.when(section == 1)
+                def _():
+                    ring_end(out_hop)
+
+        @pl.when(i >= 2)
+        def _():
+            wait_y(m, ahead)
+
         project_out(m, ahead)
-        pl.when(i == NX - 2)(lambda: pass_on(1))
-        lax.fori_loop(ended(i - 1), ended(i), stage_end, 0)
-        return carry
-
-    lax.fori_loop(0, MICRO * (NX - 1), stage_out, 0)
+        pl.when(
+            jnp.logical_or(i == jnp.where(section == 0, 1, 0), i == 4)
+        )(lambda: pass_on(jnp.where(i == 4, 1, 0)))
+
+        def end(k, carry):
+            finish(*unit(k))
+            return carry
+
+        lax.fori_loop(ended(i - 1), ended(i), end, 0)
+
+    loop(MICRO * NX, stage_out)
 
     @pl.when(section == 0)
     def _():
@@ -710,56 +791,56 @@
 
         lax.fori_loop(0, MICRO * NX, later, 0)
 
-    def drain(m, carry):
-        for ahead in (1, 2, 3):
+    def drain(m):
+        def outs(k):
             for half in range(2):
-                send_out(m, ahead, half).wait()
-        for direction in range(2):
+                send_out(m, k + 1, half).wait()
+
+        loop(NX - 1, outs)
+
+        def ways(direction):
             for half in range(2):
                 send_part(m, direction, half).wait_send()
                 send_y(m, direction, half).wait_send()
-            send_hop(m, direction).wait_send()
+            pl.when(section == 0)(lambda: send_hop(m, direction).wait_send())
             pass_y(m, direction).wait_send()
-        for ahead in range(NX):
-            for dy in (1, 2, 3):
-                send_proj(m, ahead, dy).wait_send()
+
+        loop(2, ways)
+        pl.when(section == 1)(lambda: send_far(m).wait_send())
+        loop(
+            NX * (NY - 1),
+            lambda k: send_proj(m, k // (NY - 1), k % (NY - 1) + 1).wait_send(),
+        )
 
         @pl.when(section == 0)
         def _():
-            for ahead in range(NX):
-                for dy in range(NY):
-                    onward(m, ahead, dy).wait_send()
-                    if ahead or dy:
-                        first(m, ahead, dy).wait_send()
-
-        return carry
-
-    lax.fori_loop(0, MICRO, drain, 0)
-    ring_drain(in_hop)
+            loop(NX * NY, lambda k: onward(m, k // NY, k % NY).wait_send())
+
+    loop(MICRO, drain)
+    loop(MICRO * 2, lambda k: keep(k // 2, k % 2).wait())
 
     @pl.when(section == 0)
     def _():
+        plane(lambda m, dx, dy: first(m, dx, dy).wait_send())
+
+    @pl.when(section == 0)
+    def _():
+        ring_drain(in_hop)
         own_out().wait_send()
 
-    @pl.when(section == 1)
-    def _():
-        ring_drain(relay_hop)
-        ring_drain(out_hop)
-        for step in range(1, NZ):
-            push(step).wait_send()
+    pl.when(section == 1)(lambda: ring_drain(out_hop))
 
 
 def body(
     stream, norm_gain, w_x, w_bc, w_dt, conv_x, conv_bc, dt_bias, decay_rate, skip_d, y_gain, w_out
 ):
-    vmem = pl.BlockSpec(memory_space=pltpu.VMEM)
     whole = pl.BlockSpec(memory_space=pltpu.HBM)
     dma = pltpu.SemaphoreType.DMA
     return pl.pallas_call(
         kernel,
         out_shape=jax.ShapeDtypeStruct((1, MICRO, 1, LEN, WIDTH), BF16),
         in_specs=[whole] * 12,
-        out_specs=vmem,
+        out_specs=whole,
         scratch_shapes=[
             pltpu.VMEM((MICRO, NX, LEN, 2 * LEN), BF16),
             pltpu.VMEM((1, NX * WIDTH), F32),
@@ -777,6 +858,7 @@
             pltpu.VMEM((MICRO, ROWS, COLS), BF16),
             pltpu.VMEM((MICRO, 2, LEN, COLS), BF16),
             pltpu.VMEM((MICRO, 2, HALF, COLS), BF16),
+            pltpu.VMEM((MICRO, LEN, COLS), BF16),
             pltpu.VMEM((8 + LEN, LEN), F32),
             pltpu.VMEM((LEN, WIDTH + BC), F32),
             pltpu.VMEM((LEN, WIDTH), F32),
@@ -797,6 +879,8 @@
             dma((MICRO, NX, NY)),
             dma((MICRO, 2)),
             dma((MICRO, 2)),
+            dma((MICRO,)),
+            dma((MICRO,)),
             dma((MICRO, 2, 2)),
             dma((MICRO, 2, 2)),
             dma((MICRO, 2, 2)),
@@ -815,6 +899,7 @@
             dma,
             dma((11,)),
             dma((MICRO, NX, 2)),
+            dma((MICRO, 2)),
             pltpu.SemaphoreType.REGULAR,
         ],
         compiler_params=pltpu.CompilerParams(

time: 115 us -> 113 us (0.983)
  Pallas kernels: 113 us -> 111 us
    pallas_call x1, Pallas kernels: 113 us -> 111 us  [body(): pl.pallas_call(kernel, out_shape=jax.ShapeDtypeStruct((1, MICRO, 1, LEN,...]
where the time goes in v4:
time: 113 us
  Pallas kernels  111 us (98%)
  local copies, waits for them, and re-layouts  1.87 us (2%)
    pallas_call x1, Pallas kernels, body(): pl.pallas_call(kernel, out_shape=jax.ShapeDtypeStruct((1, MICRO, 1, LEN,...  111 us

profile of v4, /device:TPU:1, one launch (start us, length us, event | category | flops | bytes accessed | tf_op | source)
XLA Modules:
  0.0 113.0 jit_solution(16572785158067933101)
XLA Ops:
  0.0 111.2 %mixer.1 = bf16[1,2,1,128,1024]{4,3,2,1,0:T(8,128)(2,1)} custom-call(bf16[2,1,128,1024]{3,2,1,0:T(8,128)(2,1)} %stream_ref.1, f32[1,4096]{1,0:T(1,128)} %gain_ref.1, bf16[1,128,1024]{2,1,0:T(8,128)(2,1)} %w_x_ref.1, bf16[1,128,256]{2,1,0:T(8,128)(2,1)} %w_bc_ref.1, bf16[1,16,128]{2,1,0:T(8,128)(2,1)} %bitcast.1, f32[1,4,1024]{2,1,0:T(4,128)} %conv_x_ref.1, ...), custom_call_target="tpu_custom_call" | custom-call | tf_op jit(solution)/shard_map/mixer/pallas_call | solution.py:839
  111.2 1.9 %copy.14 = bf16[1,2,1,128,1024]{4,3,2,1,0:T(8,128)(2,1)} copy(bf16[1,2,1,128,1024]{4,3,2,1,0:T(8,128)(2,1)} %mixer.1) | data formatting | bytes 1048576

commit v5 on v4

--- a/solution.py
+++ b/solution.py
@@ -610,7 +610,7 @@
 
     def project_out(m, ahead):
         values = y_all[m, (x + ahead) % NX]
-        for dy in (1, 3, 2, 0):
+        for dy in (2, 1, 3, 0):
             to_y = (y + dy) % NY
             cols = pl.ds(pl.multiple_of(to_y * 2 * LEN, 2 * LEN), 2 * LEN)
             proj[m, to_y, block(ahead), :] = jnp.dot(
@@ -650,7 +650,7 @@
 
         @pl.when(section == 0)
         def _():
-            for dy in (1, 3, 2, 0):
+            for dy in (2, 1, 3, 0):
                 onward(m, ahead, dy).start()
 
         pl.when(section == 1)(lambda: give(m, ahead))

time: 113 us -> 113 us (level)
  no operation moved by 1% of the time
where the time goes in v5:
time: 113 us
  Pallas kernels  111 us (98%)
  local copies, waits for them, and re-layouts  1.87 us (2%)
    pallas_call x1, Pallas kernels, body(): pl.pallas_call(kernel, out_shape=jax.ShapeDtypeStruct((1, MICRO, 1, LEN,...  111 us

profile of v5, /device:TPU:1, one launch (start us, length us, event | category | flops | bytes accessed | tf_op | source)
XLA Modules:
  0.0 112.6 jit_solution(5816852349352366453)
XLA Ops:
  0.0 110.7 %mixer.1 = bf16[1,2,1,128,1024]{4,3,2,1,0:T(8,128)(2,1)} custom-call(bf16[2,1,128,1024]{3,2,1,0:T(8,128)(2,1)} %stream_ref.1, f32[1,4096]{1,0:T(1,128)} %gain_ref.1, bf16[1,128,1024]{2,1,0:T(8,128)(2,1)} %w_x_ref.1, bf16[1,128,256]{2,1,0:T(8,128)(2,1)} %w_bc_ref.1, bf16[1,16,128]{2,1,0:T(8,128)(2,1)} %bitcast.1, f32[1,4,1024]{2,1,0:T(4,128)} %conv_x_ref.1, ...), custom_call_target="tpu_custom_call" | custom-call | tf_op jit(solution)/shard_map/mixer/pallas_call | solution.py:839
  110.7 1.9 %copy.14 = bf16[1,2,1,128,1024]{4,3,2,1,0:T(8,128)(2,1)} copy(bf16[1,2,1,128,1024]{4,3,2,1,0:T(8,128)(2,1)} %mixer.1) | data formatting | bytes 1048576
